TPU v7x, 32 devices: a whole 2x2x4 slice. The times are simulated.
32 devices in a mesh: seq: 4 (over z), dp: 8 (over y, x, core).
Axes of the slice: x: 2, y: 2, z: 4, core: 2. Of those that a mesh axis runs over, the one named last changes fastest.
Arguments:
- hidden_states: bfloat16 [8, 3072, 768], P('dp', 'seq'), may hold values from -6 to 6
- output_cotangent: bfloat16 [8, 3072, 768], P('dp', 'seq'), may hold values from -6 to 6
- document_lengths: int32 [8, 5], P('dp'), may hold values from 1 to 3068, as said below
- bucket_index: int32 [8, 24, 3072], P('dp', 'seq'), may hold values from 0 to 31
- norm_gains: float32 [2, 768], replicated, may hold values from 0.2 to 5.4
- bias_table: float32 [32, 12], replicated, may hold values from -4 to 4
- project_weight: float32 [768, 2304], P(('seq', 'dp')), may hold values from -0.21875 to 0.21875
- output_weight: float32 [768, 768], P(('seq', 'dp')), may hold values from -0.875 to 0.875
- expand_weight: float32 [768, 3072], P(('seq', 'dp')), may hold values from -0.21875 to 0.21875
- reduce_weight: float32 [3072, 768], P(('seq', 'dp')), may hold values from -0.109375 to 0.109375
- project_rows: float32 [768], P(('seq', 'dp')), may hold values from 0.1 to 3
- project_columns: float32 [2304], replicated, may hold values from 0.1 to 3
- output_rows: float32 [768], P(('seq', 'dp')), may hold values from 0.1 to 3
- output_columns: float32 [768], replicated, may hold values from 0.1 to 3
- expand_rows: float32 [768], P(('seq', 'dp')), may hold values from 0.1 to 3
- expand_columns: float32 [3072], replicated, may hold values from 0.1 to 3
- reduce_rows: float32 [3072], P(('seq', 'dp')), may hold values from 0.1 to 3
- reduce_columns: float32 [768], replicated, may hold values from 0.1 to 3
- gains_moment: float32 [2, 768], replicated, may hold values from 0.1 to 3
- table_moment: float32 [32, 12], replicated, may hold values from 0.1 to 3
Outputs:
- layer_output: bfloat16 [8, 3072, 768], P('dp', 'seq')
- input_gradient: bfloat16 [8, 3072, 768], P('dp', 'seq')
- gains_gradient: float32 [2, 768], replicated
- table_gradient: float32 [32, 12], replicated
- project_gradient: float32 [768, 2304], P(('seq', 'dp'))
- output_gradient: float32 [768, 768], P(('seq', 'dp'))
- expand_gradient: float32 [768, 3072], P(('seq', 'dp'))
- reduce_gradient: float32 [3072, 768], P(('seq', 'dp'))
- gains_updated: float32 [2, 768], replicated
- table_updated: float32 [32, 12], replicated
- project_updated: float32 [768, 2304], P(('seq', 'dp'))
- output_updated: float32 [768, 768], P(('seq', 'dp'))
- expand_updated: float32 [768, 3072], P(('seq', 'dp'))
- reduce_updated: float32 [3072, 768], P(('seq', 'dp'))
- project_rows_new: float32 [768], P(('seq', 'dp'))
- project_columns_new: float32 [2304], replicated
- output_rows_new: float32 [768], P(('seq', 'dp'))
- output_columns_new: float32 [768], replicated
- expand_rows_new: float32 [768], P(('seq', 'dp'))
- expand_columns_new: float32 [3072], replicated
- reduce_rows_new: float32 [3072], P(('seq', 'dp'))
- reduce_columns_new: float32 [768], replicated
- gains_moment_new: float32 [2, 768], replicated
- table_moment_new: float32 [32, 12], replicated
Inputs may be any that keep to these rules, and one draw needn't show every extreme that they name: `document_lengths`: each row's 5 lengths sum to 3072.
All inputs are finite; a program needn't handle non-finite values.
Results may differ from a plain program's by a relative error of at most 0.018.
The roundings to bfloat16 on the way count: a program that leaves them out, or rounds other values in their place, can miss the bound.
Values may be sent and summed in bfloat16 or wider, within the bound.
A program may use at most 192 MiB of HBM per device.

v0:
```python
import math

import jax
import jax.numpy as jnp
from jax import lax
from jax.sharding import PartitionSpec as P

D = 768
HEADS = 12
HEAD = 64
BLK = 128


score_scale = 0.125
masked_score = -1e30
norm_epsilon = 1e-06
tiny_term = 1e-30
learn_rate = 0.3
decay_rate = 1.0 - 2.0 ** (-0.8)
key_step = 128


def rms_norm(values, gain_vector):
    return (
        values
        * lax.rsqrt(jnp.mean(values * values, axis=-1, keepdims=True) + norm_epsilon)
        * gain_vector
    )


def gelu_tanh(values):
    return (
        0.5
        * values
        * (1.0 + jnp.tanh(0.7978845608028654 * (values + 0.044715 * values * values * values)))
    )


def documents(lengths, row_length):
    doc_ends = jnp.cumsum(lengths)
    position = jnp.arange(row_length, dtype=jnp.int32)
    return jnp.sum((position[:, None] >= doc_ends[None, :]).astype(jnp.int32), axis=1)


def matmul(former, latter):
    return jnp.dot(former, latter, preferred_element_type=jnp.float32)


def matmul_left(former, latter):
    return lax.dot_general(
        former, latter, (((0,), (0,)), ((), ())), preferred_element_type=jnp.float32
    )


def matmul_right(former, latter):
    return lax.dot_general(
        former, latter, (((1,), (1,)), ((), ())), preferred_element_type=jnp.float32
    )


def key_blocks():
    return key_step


def block_bias(bucket_rows, bias_table, key_start, amount):
    picked = lax.dynamic_slice_in_dim(bucket_rows, key_start, amount, 1)
    one_hot = (
        picked[:, :, None] == jnp.arange(bias_table.shape[0], dtype=jnp.int32)[None, None, :]
    ).astype(jnp.float32)
    bias_block = jnp.einsum("qkb,bh->hqk", one_hot, bias_table, precision=lax.Precision.HIGHEST)
    return (one_hot, bias_block)


def block_scores(queries, key_block, bias_block, same_doc):
    raw_scores = jnp.einsum("qhe,khe->hqk", queries, key_block, preferred_element_type=jnp.float32)
    heads_count, query_count, amount = raw_scores.shape
    shaped = (raw_scores * score_scale).reshape(
        heads_count, query_count // BLK, BLK, amount
    ) + bias_block[:, :, None, :]
    return jnp.where(same_doc[None], shaped.reshape(heads_count, query_count, amount), masked_score)


def attend_range(
    soft_state, key_rows, value_rows, queries, doc_query, doc_all, bucket_rows, bias_table
):
    block_rows = key_blocks()

    def attend_block(block_index, loop_carry):
        running_max, running_sum, weighted = loop_carry
        offset = block_index * block_rows
        key_block = lax.dynamic_slice_in_dim(key_rows, offset, block_rows, 0).reshape(
            block_rows, HEADS, HEAD
        )
        value_block = lax.dynamic_slice_in_dim(value_rows, offset, block_rows, 0).reshape(
            block_rows, HEADS, HEAD
        )
        one_hot, bias_block = block_bias(bucket_rows, bias_table, offset, block_rows)
        same_doc = (
            doc_query[:, None] == lax.dynamic_slice_in_dim(doc_all, offset, block_rows)[None, :]
        )
        scores = block_scores(queries, key_block, bias_block, same_doc)
        new_max = jnp.maximum(running_max, jnp.max(scores, axis=-1))
        fading = jnp.exp(running_max - new_max)
        unscaled = jnp.exp(scores - new_max[:, :, None])
        running_sum = running_sum * fading + jnp.sum(unscaled, axis=-1)
        weighted = weighted * fading[:, :, None] + jnp.einsum(
            "hqk,khe->hqe",
            unscaled.astype(jnp.bfloat16),
            value_block,
            preferred_element_type=jnp.float32,
        )
        return (new_max, running_sum, weighted)

    return lax.fori_loop(0, key_rows.shape[0] // block_rows, attend_block, soft_state)


def body(
    hidden_states,
    output_cotangent,
    document_lengths,
    bucket_index,
    norm_gains,
    bias_table,
    project_weight,
    output_weight,
    expand_weight,
    reduce_weight,
    project_rows,
    project_columns,
    output_rows,
    output_columns,
    expand_rows,
    expand_columns,
    reduce_rows,
    reduce_columns,
    gains_moment,
    table_moment,
):
    local_rows = hidden_states.shape[1]
    row_length = local_rows * lax.axis_size("seq")
    gradient_scale = 1.0 / math.sqrt(row_length * lax.axis_size("dp"))
    shards = (
        project_weight.astype(jnp.bfloat16),
        output_weight.astype(jnp.bfloat16),
        expand_weight.astype(jnp.bfloat16),
        reduce_weight.astype(jnp.bfloat16),
    )
    gathered = (
        lax.all_gather(shards[0], ("seq", "dp"), axis=0, tiled=True),
        lax.all_gather(shards[1], ("seq", "dp"), axis=0, tiled=True),
        lax.all_gather(shards[2], ("seq", "dp"), axis=0, tiled=True),
        lax.all_gather(shards[3], ("seq", "dp"), axis=0, tiled=True),
    )
    project_full, output_full, expand_full, reduce_full = gathered
    doc_all = documents(document_lengths[0], row_length)
    doc_query = lax.dynamic_slice_in_dim(doc_all, lax.axis_index("seq") * local_rows, local_rows)
    bucket_rows = bucket_index[0]
    inputs = hidden_states[0].astype(jnp.float32)
    normed_one, pullback_one = jax.vjp(rms_norm, inputs, norm_gains[0])
    normed_low = normed_one.astype(jnp.bfloat16)
    projected = matmul(normed_low, project_full).astype(jnp.bfloat16)
    queries = projected[:, :D].reshape(local_rows, HEADS, HEAD)
    key_rows = projected[:, D : 2 * D]
    value_rows = projected[:, 2 * D :]
    start_state = (
        jnp.full((HEADS, local_rows), masked_score, jnp.float32),
        jnp.zeros((HEADS, local_rows), jnp.float32),
        jnp.zeros((HEADS, local_rows, HEAD), jnp.float32),
    )
    soft_state = attend_range(
        start_state,
        lax.all_gather(key_rows, "seq", axis=0, tiled=True),
        lax.all_gather(value_rows, "seq", axis=0, tiled=True),
        queries,
        doc_query,
        doc_all,
        bucket_rows,
        bias_table,
    )
    running_max, running_sum, weighted = soft_state
    context_heads = weighted / running_sum[:, :, None]
    log_total = running_max + jnp.log(running_sum)
    context_low = (
        jnp.transpose(context_heads, (1, 0, 2)).reshape(local_rows, D).astype(jnp.bfloat16)
    )
    residual = inputs + matmul(context_low, output_full)
    normed_two, pullback_two = jax.vjp(rms_norm, residual, norm_gains[1])
    normed_two_low = normed_two.astype(jnp.bfloat16)
    expanded = matmul(normed_two_low, expand_full)
    activated, pullback_gelu = jax.vjp(gelu_tanh, expanded)
    activated_low = activated.astype(jnp.bfloat16)
    layer_output = (residual + matmul(activated_low, reduce_full)).astype(jnp.bfloat16)[None]
    upstream = output_cotangent[0].astype(jnp.float32)
    upstream_low = upstream.astype(jnp.bfloat16)
    reduce_term = matmul_left(activated_low, upstream_low)
    (expanded_grad,) = pullback_gelu(matmul_right(upstream_low, reduce_full))
    expanded_low = expanded_grad.astype(jnp.bfloat16)
    expand_term = matmul_left(normed_two_low, expanded_low)
    residual_part, gain_two_grad = pullback_two(matmul_right(expanded_low, expand_full))
    residual_grad = upstream + residual_part
    residual_low = residual_grad.astype(jnp.bfloat16)
    output_term = matmul_left(context_low, residual_low)
    context_grad = (
        matmul_right(residual_low, output_full)
        .astype(jnp.bfloat16)
        .reshape(local_rows, HEADS, HEAD)
    )
    delta_sum = jnp.einsum("qhe,hqe->hq", context_grad.astype(jnp.float32), context_heads)
    whole_keys, whole_values = (
        lax.all_gather(key_rows, "seq", axis=0, tiled=True),
        lax.all_gather(value_rows, "seq", axis=0, tiled=True),
    )
    block_rows = key_blocks()

    def back_block(block_index, loop_carry):
        query_grad, table_grad, key_terms = loop_carry
        offset = block_index * block_rows
        key_block = lax.dynamic_slice_in_dim(whole_keys, offset, block_rows, 0).reshape(
            block_rows, HEADS, HEAD
        )
        value_block = lax.dynamic_slice_in_dim(whole_values, offset, block_rows, 0).reshape(
            block_rows, HEADS, HEAD
        )
        one_hot, bias_block = block_bias(bucket_rows, bias_table, offset, block_rows)
        same_doc = (
            doc_query[:, None] == lax.dynamic_slice_in_dim(doc_all, offset, block_rows)[None, :]
        )
        scores = block_scores(queries, key_block, bias_block, same_doc)
        attention = jnp.exp(scores - log_total[:, :, None])
        attention_grad = jnp.einsum(
            "qhe,khe->hqk", context_grad, value_block, preferred_element_type=jnp.float32
        )
        score_grad = attention * (attention_grad - delta_sum[:, :, None])
        folded = jnp.sum(score_grad.reshape(HEADS, local_rows // BLK, BLK, block_rows), axis=2)
        table_grad = table_grad + jnp.einsum(
            "hqk,qkb->bh", folded, one_hot, precision=lax.Precision.HIGHEST
        )
        score_low = (score_grad * score_scale).astype(jnp.bfloat16)
        query_grad = query_grad + jnp.einsum(
            "hqk,khe->qhe", score_low, key_block, preferred_element_type=jnp.float32
        )
        key_grad = jnp.einsum(
            "hqk,qhe->khe", score_low, queries, preferred_element_type=jnp.float32
        ).reshape(block_rows, D)
        value_grad = jnp.einsum(
            "hqk,qhe->khe",
            attention.astype(jnp.bfloat16),
            context_grad,
            preferred_element_type=jnp.float32,
        ).reshape(block_rows, D)
        key_terms = lax.dynamic_update_slice_in_dim(
            key_terms, jnp.concatenate([key_grad, value_grad], axis=1), offset, 0
        )
        return (query_grad, table_grad, key_terms)

    back_start = (
        jnp.zeros((local_rows, HEADS, HEAD), jnp.float32),
        jnp.zeros(bias_table.shape, jnp.float32),
        jnp.zeros((row_length, 2 * D), jnp.float32),
    )
    query_grad, table_grad, key_terms = lax.fori_loop(
        0, row_length // block_rows, back_block, back_start
    )
    key_sums = lax.psum_scatter(
        key_terms.astype(jnp.bfloat16), "seq", scatter_dimension=0, tiled=True
    ).astype(jnp.float32)
    projected_grad = jnp.concatenate([query_grad.reshape(local_rows, D), key_sums], axis=1).astype(
        jnp.bfloat16
    )
    project_term = matmul_left(normed_low, projected_grad)
    input_part, gain_one_grad = pullback_one(matmul_right(projected_grad, project_full))
    input_gradient = (residual_grad + input_part).astype(jnp.bfloat16)[None]
    full_terms = (project_term, output_term, expand_term, reduce_term)
    shares = (
        lax.psum_scatter(full_terms[0], ("seq", "dp"), scatter_dimension=0, tiled=True),
        lax.psum_scatter(full_terms[1], ("seq", "dp"), scatter_dimension=0, tiled=True),
        lax.psum_scatter(full_terms[2], ("seq", "dp"), scatter_dimension=0, tiled=True),
        lax.psum_scatter(full_terms[3], ("seq", "dp"), scatter_dimension=0, tiled=True),
    )
    gradients = tuple((share * gradient_scale for share in shares))
    row_before = (project_rows, output_rows, expand_rows, reduce_rows)
    row_after = []
    column_parts = []
    row_sums = []
    for gradient, previous in zip(gradients, row_before):
        squares = gradient * gradient + tiny_term
        updated_rows = decay_rate * previous + (1.0 - decay_rate) * jnp.mean(squares, axis=1)
        row_after.append(updated_rows)
        column_parts.append(jnp.sum(squares, axis=0))
        row_sums.append(jnp.sum(updated_rows))
    summed = lax.psum(
        (
            column_parts[0],
            column_parts[1],
            column_parts[2],
            column_parts[3],
            jnp.stack(row_sums),
            jnp.stack([gain_one_grad, gain_two_grad]),
            table_grad,
        ),
        ("seq", "dp"),
    )
    column_before = (project_columns, output_columns, expand_columns, reduce_columns)
    weights_before = (project_weight, output_weight, expand_weight, reduce_weight)
    full_rows = (
        project_full.shape[0],
        output_full.shape[0],
        expand_full.shape[0],
        reduce_full.shape[0],
    )
    updated_weights = []
    columns_after = []
    for position in range(4):
        columns_new = decay_rate * column_before[position] + (1.0 - decay_rate) * (
            summed[position] / full_rows[position]
        )
        row_mean = summed[4][position] / full_rows[position]
        denominator = row_after[position][:, None] * columns_new[None, :] / row_mean
        updated_weights.append(
            weights_before[position] - learn_rate * gradients[position] * lax.rsqrt(denominator)
        )
        columns_after.append(columns_new)
    gains_gradient = summed[5] * gradient_scale
    table_gradient = summed[6] * gradient_scale
    gains_moment_new = decay_rate * gains_moment + (1.0 - decay_rate) * (
        gains_gradient * gains_gradient + tiny_term
    )
    gains_updated = norm_gains - learn_rate * gains_gradient * lax.rsqrt(gains_moment_new)
    table_moment_new = decay_rate * table_moment + (1.0 - decay_rate) * (
        table_gradient * table_gradient + tiny_term
    )
    table_updated = bias_table - learn_rate * table_gradient * lax.rsqrt(table_moment_new)
    return (
        layer_output,
        input_gradient,
        gains_gradient,
        table_gradient,
        gradients[0],
        gradients[1],
        gradients[2],
        gradients[3],
        gains_updated,
        table_updated,
        updated_weights[0],
        updated_weights[1],
        updated_weights[2],
        updated_weights[3],
        row_after[0],
        columns_after[0],
        row_after[1],
        columns_after[1],
        row_after[2],
        columns_after[2],
        row_after[3],
        columns_after[3],
        gains_moment_new,
        table_moment_new,
    )


def solution(mesh):
    placed = (
        P("dp", "seq", None),
        P("dp", "seq", None),
        P("dp", None),
        P("dp", "seq", None),
        P(),
        P(),
        P(("seq", "dp"), None),
        P(("seq", "dp"), None),
        P(("seq", "dp"), None),
        P(("seq", "dp"), None),
        P(("seq", "dp")),
        P(),
        P(("seq", "dp")),
        P(),
        P(("seq", "dp")),
        P(),
        P(("seq", "dp")),
        P(),
        P(),
        P(),
    )
    return jax.shard_map(
        body,
        mesh=mesh,
        in_specs=placed,
        out_specs=(
            P("dp", "seq", None),
            P("dp", "seq", None),
            P(),
            P(),
            P(("seq", "dp"), None),
            P(("seq", "dp"), None),
            P(("seq", "dp"), None),
            P(("seq", "dp"), None),
            P(),
            P(),
            P(("seq", "dp"), None),
            P(("seq", "dp"), None),
            P(("seq", "dp"), None),
            P(("seq", "dp"), None),
            P(("seq", "dp")),
            P(),
            P(("seq", "dp")),
            P(),
            P(("seq", "dp")),
            P(),
            P(("seq", "dp")),
            P(),
            P(),
            P(),
        ),
        check_vma=False,
    )
```

profile of v0, /device:TPU:0, one launch (start us, length us, event | category | flops | bytes accessed | tf_op | source)
XLA Modules:
  0.0 2292.2 jit_solution(17398038846457208719)
XLA Ops:
  10.9 63.4 %all-gather.7.cloned.1.call-done = bf16[768,2304]{1,0:T(8,128)(2,1)} async-done(((bf16[24,2304]{1,0:T(8,128)(2,1)}), bf16[768,2304]{1,0:T(8,128)(2,1)}) %all-gather.7.cloned.1.call-update) | async-done | bytes 3538960 | tf_op jit(solution)/shard_map/all_gather | solution.py:149
  91.3 78.7 %all-gather.11.cloned.1.call-done = bf16[3072,768]{1,0:T(8,128)(2,1)} async-done(((bf16[768,768]{1,0:T(8,128)(2,1)}), bf16[3072,768]{1,0:T(8,128)(2,1)}) %all-gather.11.cloned.1.call-update) | async-done | bytes 4718608 | tf_op jit(solution)/shard_map/all_gather | solution.py:173
  170.0 6.6 copy.125
  176.6 82.8 %all-gather.9.cloned.1.call-done = bf16[3072,768]{1,0:T(8,128)(2,1)} async-done(((bf16[768,768]{1,0:T(8,128)(2,1)}), bf16[3072,768]{1,0:T(8,128)(2,1)}) %all-gather.9.cloned.1.call-update) | async-done | bytes 4718608 | tf_op jit(solution)/shard_map/all_gather | solution.py:172
  259.5 6.6 copy.124
  266.1 465.2 %while.36 = (s32[]{:T(128)}, f32[12,768]{1,0:T(8,128)}, f32[12,768]{1,0:T(8,128)}, f32[12,768,64]{1,2,0:T(8,128)S(1)}, s32[768]{0:T(1024)S(1)}, /*index=5*/s32[3...) while((s32[]{:T(128)}, f32[12,768]{1,0:T(8,128)}, ...), condition=%wide.region_6.7_spmd.clone, body=%wide.region_3.6_spmd.clone.sunk | while | flops 316904448 | bytes 42286408 | solution.py:114
  292.1 6.1 copy.161
  311.5 6.1 copy.161
  330.9 6.1 copy.161
  350.3 6.1 copy.161
  369.7 6.2 copy.161
  389.2 6.2 copy.161
  408.6 6.1 copy.161
  428.0 6.1 copy.161
  563.6 6.1 copy.161
  583.0 6.1 copy.161
  602.4 6.1 copy.161
  621.7 6.1 copy.161
  739.2 10.7 fusion.70
  749.9 14.3 fusion.28
  778.1 779.5 %while.37 = (s32[]{:T(128)}, f32[768,12,64]{0,2,1:T(8,128)}, f32[32,12]{0,1:T(8,128)S(1)}, bf16[3072,1536]{0,1:T(8,128)(2,1)}, bf16[3072,768]{0,1:T(8,128)(2,1)}...) while((s32[]{:T(128)}, f32[768,12,64]{0,2,1:T(8,128)}, ...), condition=%wide.region_11.12_spmd.clone, body=%wide.region_9.11_spmd.clone.sunk | while | flops 778313472 | bytes 92722448 | solution.py:261
  1564.4 10.1 fusion.45
  1575.2 10.6 fusion.69
  1589.1 129.5 %reduce-scatter.6.cloned.1.call-done = bf16[768,1536]{0,1:T(8,128)(2,1)} async-done(((bf16[3072,1536]{0,1:T(8,128)(2,1)}), bf16[768,1536]{0,1:T(8,128)(2,1)}) %reduce-scatter.6.cloned.1.call-update) | async-done | bytes 2359312 | tf_op jit(solution)/shard_map/reduce_scatter | solution.py:264
  1718.6 7.9 fusion.41
  1727.8 10.8 fusion.43
  1741.0 82.7 %reduce-scatter.10.cloned.1.call-done = f32[24,768]{1,0:T(8,128)} async-done(((f32[768,768]{1,0:T(8,128)}), f32[24,768]{1,0:T(8,128)}) %reduce-scatter.10.cloned.1.call-update) | async-done | bytes 73744 | tf_op jit(solution)/shard_map/reduce_scatter | solution.py:276
  1826.9 138.4 %reduce-scatter.14.cloned.1.call-done = f32[96,768]{1,0:T(8,128)} async-done(((f32[3072,768]{1,0:T(8,128)}), f32[96,768]{1,0:T(8,128)}) %reduce-scatter.14.cloned.1.call-update) | async-done | bytes 294928 | tf_op jit(solution)/shard_map/reduce_scatter | solution.py:278
  1968.9 136.5 %reduce-scatter.12.cloned.1.call-done = f32[24,3072]{1,0:T(8,128)} async-done(((f32[768,3072]{1,0:T(8,128)}), f32[24,3072]{1,0:T(8,128)}) %reduce-scatter.12.cloned.1.call-update) | async-done | bytes 294928 | tf_op jit(solution)/shard_map/reduce_scatter | solution.py:277
  2109.5 6.2 fusion.34
  2120.9 109.7 %reduce-scatter.8.cloned.1.call-done = f32[24,2304]{1,0:T(8,128)} async-done(((f32[768,2304]{1,0:T(8,128)}), f32[24,2304]{1,0:T(8,128)}) %reduce-scatter.8.cloned.1.call-update) | async-done | bytes 221200 | tf_op jit(solution)/shard_map/reduce_scatter | solution.py:275
  2235.6 41.1 %all-reduce = (f32[2,768]{1,0:T(2,128)S(1)}, f32[32,12]{0,1:T(8,128)S(1)}, f32[4]{0:T(128)S(1)}, f32[2304]{0:T(1024)S(1)}, f32[768]{0:T(1024)S(1)}, /*index=5*/f32[3072]{0:T(1024)S(1)}, f32[768]{0:T(1024)S(1)}) all-reduce(f32[2,768]{1,0:T(2,128)S(1)} %pad_maximum_fusion.3, ...), channel_id=1, replica_groups=mesh['seq'=4,'dp'=8] {'seq','dp'}, use_global_device_ids=true, to_apply=%region_16.17 | all-reduce | flops 8836 | bytes 70688 | tf_op jit(solution)/shard_map/psum | solution.py:291
  (1192 shorter events, 1250.5 us)
Async XLA Ops:
  7.2 67.1 %all-gather.7.cloned.1.call-start = ((), (), s32[]{:S(2)}) async-start(), calls=%async_computation.5 | async-start | bytes 3649536 | tf_op jit(solution)/shard_map/all_gather | solution.py:149
  8.9 161.1 %all-gather.11.cloned.1.call-start = ((), (), s32[]{:S(2)}) async-start(), calls=%async_computation.7 | async-start | bytes 5898240 | tf_op jit(solution)/shard_map/all_gather | solution.py:173
  81.6 177.8 %all-gather.9.cloned.1.call-start = ((), (), s32[]{:S(2)}) async-start(), calls=%async_computation.6 | async-start | bytes 5898240 | tf_op jit(solution)/shard_map/all_gather | solution.py:172
  82.4 651.0 %all-gather.13.cloned.1.call-start = ((), (), s32[]{:S(2)}) async-start(), calls=%async_computation.8 | async-start | bytes 1216512 | tf_op jit(solution)/shard_map/all_gather | solution.py:150
  83.1 656.1 %all-gather.15.cloned.1.call-start = ((), (), s32[]{:S(2)}) async-start(), calls=%async_computation.9 | async-start | bytes 4866048 | tf_op jit(solution)/shard_map/all_gather | solution.py:151
  83.9 666.0 %all-gather.17.cloned.1.call-start = ((), (), s32[]{:S(2)}) async-start(), calls=%async_computation.10 | async-start | bytes 4866048 | tf_op jit(solution)/shard_map/all_gather | solution.py:152
  84.6 1634.0 %reduce-scatter.6.cloned.1.call-start = ((), (), s32[]{:S(2)}) async-start(), calls=%async_computation.11 | async-start | bytes 11796480 | tf_op jit(solution)/shard_map/reduce_scatter | solution.py:264
  1558.3 265.4 %reduce-scatter.10.cloned.1.call-start = ((), (), s32[]{:S(2)}) async-start(), calls=%async_computation.13 | async-start | bytes 2433024 | tf_op jit(solution)/shard_map/reduce_scatter | solution.py:276
  1562.8 402.5 %reduce-scatter.14.cloned.1.call-start = ((), (), s32[]{:S(2)}) async-start(), calls=%async_computation.15 | async-start | bytes 9732096 | tf_op jit(solution)/shard_map/reduce_scatter | solution.py:278
  1574.5 530.9 %reduce-scatter.12.cloned.1.call-start = ((), (), s32[]{:S(2)}) async-start(), calls=%async_computation.14 | async-start | bytes 9732096 | tf_op jit(solution)/shard_map/reduce_scatter | solution.py:277
  1585.8 132.8 %copy-start.7 = (bf16[1,768,768]{1,2,0:T(8,128)(2,1)S(1)}, bf16[1,768,768]{1,2,0:T(8,128)(2,1)}, u32[]{:S(2)}) copy-start(bf16[1,768,768]{1,2,0:T(8,128)(2,1)} %copy-done.6) | copy-start | bytes 3538948
  1585.8 132.8 %copy-start.46 = (f32[768]{0:T(1024)S(1)}, f32[768]{0:T(1024)}, u32[]{:S(2)}) copy-start(f32[768]{0:T(1024)} %copy-done.45) | copy-start | bytes 9220
  1585.8 132.8 %copy-start.48 = (f32[768]{0:T(1024)S(1)}, f32[768]{0:T(1024)}, u32[]{:S(2)}) copy-start(f32[768]{0:T(1024)} %copy-done.47) | copy-start | bytes 9220
  1585.8 644.7 %reduce-scatter.8.cloned.1.call-start = ((), (), s32[]{:S(2)}) async-start(), calls=%async_computation.12 | async-start | bytes 7299072 | tf_op jit(solution)/shard_map/reduce_scatter | solution.py:275
  2118.0 117.6 %copy-start.31 = (f32[32,12]{0,1:T(8,128)S(1)}, f32[32,12]{0,1:T(8,128)}, u32[]{:S(2)}) copy-start(f32[32,12]{0,1:T(8,128)} %copy-done.30) | copy-start | bytes 4612
  2118.0 161.9 %copy-start.57 = (f32[2304]{0:T(1024)S(1)}, f32[2304]{0:T(1024)}, u32[]{:S(2)}) copy-start(f32[2304]{0:T(1024)} %param.35) | copy-start | bytes 27652
  2118.0 161.9 %copy-start.58 = (f32[3072]{0:T(1024)S(1)}, f32[3072]{0:T(1024)}, u32[]{:S(2)}) copy-start(f32[3072]{0:T(1024)} %param.39) | copy-start | bytes 36868
  2118.0 161.9 %copy-start.44 = (f32[2,768]{1,0:T(2,128)S(1)}, f32[2,768]{1,0:T(2,128)}, u32[]{:S(2)}) copy-start(f32[2,768]{1,0:T(2,128)} %param.28) | copy-start | bytes 18436
  2118.0 161.9 %copy-start.60 = (f32[2,768]{1,0:T(2,128)S(1)}, f32[2,768]{1,0:T(2,128)}, u32[]{:S(2)}) copy-start(f32[2,768]{1,0:T(2,128)} %param.42) | copy-start | bytes 18436
  2118.1 162.5 %copy-start.59 = (f32[32,12]{0,1:T(8,128)S(1)}, f32[32,12]{0,1:T(8,128)}, u32[]{:S(2)}) copy-start(f32[32,12]{0,1:T(8,128)} %param.43) | copy-start | bytes 4612
  2118.1 163.1 %copy-start.62 = (f32[768]{0:T(1024)S(1)}, f32[768]{0:T(1024)}, u32[]{:S(2)}) copy-start(f32[768]{0:T(1024)} %param.41) | copy-start | bytes 9220
  2118.1 163.1 %copy-start.63 = (f32[768]{0:T(1024)S(1)}, f32[768]{0:T(1024)}, u32[]{:S(2)}) copy-start(f32[768]{0:T(1024)} %param.37) | copy-start | bytes 9220
  2118.1 163.1 %copy-start.33 = (f32[24,768]{1,0:T(8,128)S(1)}, f32[24,768]{1,0:T(8,128)}, u32[]{:S(2)}) copy-start(f32[24,768]{1,0:T(8,128)} %param.31) | copy-start | bytes 221188
  2118.1 163.1 %copy-start.34 = (f32[24,768]{1,0:T(8,128)S(1)}, f32[24,768]{1,0:T(8,128)}, u32[]{:S(2)}) copy-start(f32[24,768]{1,0:T(8,128)} %reduce-scatter.10.cloned.1.call-done) | copy-start | bytes 221188
  2118.1 163.1 %copy-start.64 = (f32[24]{0:T(128)S(1)}, f32[24]{0:T(128)}, u32[]{:S(2)}) copy-start(f32[24]{0:T(128)} %get-tuple-element.807) | copy-start | bytes 292
  2118.1 163.9 %copy-start.22 = (f32[96,768]{1,0:T(8,128)S(1)}, f32[96,768]{1,0:T(8,128)}, u32[]{:S(2)}) copy-start(f32[96,768]{1,0:T(8,128)} %param.33) | copy-start | bytes 884740
  2118.1 163.8 %copy-start.25 = (f32[96,768]{1,0:T(8,128)S(1)}, f32[96,768]{1,0:T(8,128)}, u32[]{:S(2)}) copy-start(f32[96,768]{1,0:T(8,128)} %reduce-scatter.14.cloned.1.call-done) | copy-start | bytes 884740
  2118.2 163.8 %copy-start.65 = (f32[96]{0:T(128)S(1)}, f32[96]{0:T(128)}, u32[]{:S(2)}) copy-start(f32[96]{0:T(128)} %get-tuple-element.813) | copy-start | bytes 1156
  2118.2 164.7 %copy-start.28 = (f32[24,2304]{1,0:T(8,128)S(1)}, f32[24,2304]{1,0:T(8,128)}, u32[]{:S(2)}) copy-start(f32[24,2304]{1,0:T(8,128)} %param.30) | copy-start | bytes 663556
  2118.2 166.4 %copy-start.24 = (f32[24,3072]{1,0:T(8,128)S(1)}, f32[24,3072]{1,0:T(8,128)}, u32[]{:S(2)}) copy-start(f32[24,3072]{1,0:T(8,128)} %param.32) | copy-start | bytes 884740
  2118.2 166.4 %copy-start.26 = (f32[24,3072]{1,0:T(8,128)S(1)}, f32[24,3072]{1,0:T(8,128)}, u32[]{:S(2)}) copy-start(f32[24,3072]{1,0:T(8,128)} %reduce-scatter.12.cloned.1.call-done) | copy-start | bytes 884740
  2118.2 166.4 %copy-start.66 = (f32[24]{0:T(128)S(1)}, f32[24]{0:T(128)}, u32[]{:S(2)}) copy-start(f32[24]{0:T(128)} %get-tuple-element.810) | copy-start | bytes 292
  (167 other events, 1227.9 us)
Sparse Core Ops, SparseCore 0:
  11.5 62.7 all-gather.6
  81.8 88.2 all-gather.10
  171.6 87.8 all-gather.8
  262.2 52.4 all-gather.12
  318.1 62.5 all-gather.14
  384.0 62.4 all-gather.16
  1558.4 160.1 reduce-scatter.5
  1723.9 99.7 reduce-scatter.9
  1830.6 134.6 reduce-scatter.13
  1971.1 134.2 reduce-scatter.11
  2112.0 118.4 reduce-scatter.7
where the time goes:
time: 2310 us; the launch traced here: 2290 us
  waiting for transfers between devices  823 us (36%)
  local copies, waits for them, and re-layouts  786 us (34%)
  matrix products  458 us (20%)
  other arithmetic  163 us (7%)
  blocking collectives  41.1 us (2%)
    add x96, local copies, waits for them, and re-layouts, block_scores(): (raw_scores * score_scale).reshape(heads_count, query_count // BLK, BLK,...  410 us
    dot_general x48, matrix products, block_scores(): jnp.einsum('qhe,khe->hqk', queries, key_block, preferred_element_type=jnp...  175 us
    mul x24, local copies, waits for them, and re-layouts, back_block(): score_grad = attention * (attention_grad - delta_sum[:, :, None])  145 us
    reduce_scatter x1, waiting for transfers between devices, body(): lax.psum_scatter(full_terms[3], ('seq', 'dp'), scatter_dimension=0, tiled...  138 us
    reduce_scatter x1, waiting for transfers between devices, body(): lax.psum_scatter(full_terms[2], ('seq', 'dp'), scatter_dimension=0, tiled...  136 us
    reduce_scatter x1, waiting for transfers between devices, body(): lax.psum_scatter(key_terms.astype(jnp.bfloat16), 'seq', scatter_dimension...  130 us
    reduce_scatter x1, waiting for transfers between devices, body(): lax.psum_scatter(full_terms[0], ('seq', 'dp'), scatter_dimension=0, tiled...  110 us
    dot_general x24, matrix products, back_block(): jnp.einsum('hqk,khe->qhe', score_low, key_block, preferred_element_type=j...  84 us
  transfers between devices with their start and end apart: 11, of which 8 were waited for; matrix products, arithmetic and copies ran while one was open for 25% of the time, Pallas kernels for 0%

commit v1 on v0

v1 whole, which is shorter than its diff:
```python
import math

import jax
import jax.numpy as jnp
from jax import lax
from jax.experimental import pallas as pl
from jax.experimental.pallas import tpu as pltpu
from jax.sharding import PartitionSpec as P

D = 768
HEADS = 12
HEAD = 64
BLK = 128
PAIR = 2 * HEAD
PAIRS = HEADS // 2
DOCS = 5
TERMS = 3

score_scale = 0.125
masked_score = -1e30
norm_epsilon = 1e-06
tiny_term = 1e-30
learn_rate = 0.3
decay_rate = 1.0 - 2.0 ** (-0.8)
back_step = 768
vmem_bytes = 56 * 2**20

low_type = jnp.bfloat16
f32 = jnp.float32


def dot(former, latter, former_axis, latter_axis):
    return lax.dot_general(
        former,
        latter,
        (((former_axis,), (latter_axis,)), ((), ())),
        preferred_element_type=f32,
    )


def rms_norm(values, gain_vector):
    return (
        values
        * lax.rsqrt(jnp.mean(values * values, axis=-1, keepdims=True) + norm_epsilon)
        * gain_vector
    )


def gelu_tanh(values):
    return (
        0.5
        * values
        * (1.0 + jnp.tanh(0.7978845608028654 * (values + 0.044715 * values * values * values)))
    )


def documents(lengths, row_length):
    doc_ends = jnp.cumsum(lengths)
    position = jnp.arange(row_length, dtype=jnp.int32)
    return jnp.sum((position[:, None] >= doc_ends[None, :]).astype(jnp.int32), axis=1)


def split_terms(values):
    terms = []
    rest = values
    for _ in range(TERMS):
        term = lax.reduce_precision(rest, 8, 7)
        terms.append(term)
        rest = rest - term
    return terms


def extra_columns(blocks):
    return TERMS * blocks, TERMS * blocks + DOCS


def query_extra(doc_query, blocks):
    count = doc_query.shape[0]
    doc_start, one_start = extra_columns(blocks)
    lane = lax.broadcasted_iota(jnp.int32, (count, 128), 1)
    block = lax.broadcasted_iota(jnp.int32, (count, 128), 0) // BLK
    is_block = (lane < doc_start) & (lane % blocks == block)
    is_doc = (lane >= doc_start) & (lane < one_start) & (lane - doc_start == doc_query[:, None])
    return (is_block | is_doc).astype(low_type)


def with_row_terms(extra, values, blocks):
    _, one_start = extra_columns(blocks)
    lane = lax.broadcasted_iota(jnp.int32, (1, 1, 128), 2)
    result = jnp.broadcast_to(extra.astype(f32)[None], (HEADS,) + extra.shape)
    for place, term in enumerate(split_terms(values)):
        result = jnp.where(lane == one_start + place, term[:, :, None], result)
    return result.astype(low_type)


def key_picks(bucket_rows, doc_all, buckets):
    blocks, row_length = bucket_rows.shape
    one_hot = (
        bucket_rows.T[:, :, None] == jnp.arange(buckets, dtype=jnp.int32)[None, None, :]
    ).reshape(row_length, blocks * buckets)
    other_doc = doc_all[:, None] != jnp.arange(DOCS, dtype=jnp.int32)[None, :]
    ones = jnp.ones((row_length, 1), jnp.bool_)
    return jnp.concatenate([one_hot, other_doc, ones], axis=1).astype(low_type)


def key_extra(picks, bias_table, blocks):
    buckets = bias_table.shape[0]
    doc_start, one_start = extra_columns(blocks)
    terms = jnp.stack(split_terms(bias_table), axis=0)
    lane = jnp.arange(128, dtype=jnp.int32)
    place = jnp.clip(lane // blocks, 0, TERMS - 1)
    spread = jnp.transpose(terms[place], (1, 2, 0))
    at_block = (lane[None, :] % blocks == jnp.arange(blocks, dtype=jnp.int32)[:, None]) & (
        lane[None, :] < doc_start
    )
    bias_part = jnp.where(at_block[:, None, None, :], spread[None], 0.0).reshape(
        blocks * buckets, HEADS, 128
    )
    doc_part = jnp.where(
        lane[None, :] - doc_start == jnp.arange(DOCS, dtype=jnp.int32)[:, None], masked_score, 0.0
    )
    one_part = ((lane >= one_start) & (lane < one_start + TERMS)).astype(f32)[None]
    rest = jnp.concatenate([doc_part, one_part], axis=0)
    rest = jnp.broadcast_to(rest[:, None, :], (DOCS + 1, HEADS, 128))
    whole = jnp.concatenate([bias_part, rest], axis=0).reshape(-1, HEADS * 128).astype(low_type)
    return dot(picks, whole, 1, 0).astype(low_type)


def forward_kernel(queries, extra, keys, values_t, keys_extra, context_t, log_total):
    count = queries.shape[0]
    lane = lax.broadcasted_iota(jnp.int32, (count, PAIR), 1)
    query_pair = queries[...]
    for head in range(2):
        mine = (lane < HEAD) if head == 0 else (lane >= HEAD)
        query_side = jnp.concatenate(
            [jnp.where(mine, query_pair, jnp.zeros_like(query_pair)), extra[...]], axis=1
        )
        key_side = jnp.concatenate([keys[...], keys_extra[:, 128 * head : 128 * head + 128]], axis=1)
        scores = dot(key_side, query_side, 1, 1)
        top = jnp.max(scores, axis=0, keepdims=True)
        unscaled = jnp.exp(scores - top).astype(low_type)
        value_side = jnp.concatenate(
            [
                values_t[HEAD * head : HEAD * head + HEAD, :],
                jnp.ones((16, unscaled.shape[0]), low_type),
            ],
            axis=0,
        )
        weighted = dot(value_side, unscaled, 1, 0)
        total = weighted[HEAD : HEAD + 1]
        context_t[pl.ds(HEAD * head, HEAD), :] = weighted[:HEAD] / total
        log_total[pl.ds(8 * head, 8), :] = jnp.broadcast_to(top + jnp.log(total), (8, count))


def attend(queries, extra, keys, values_t, keys_extra):
    count, row_length = queries.shape[0], keys.shape[0]
    return pl.pallas_call(
        forward_kernel,
        grid=(PAIRS,),
        out_shape=[
            jax.ShapeDtypeStruct((D, count), f32),
            jax.ShapeDtypeStruct((HEADS * 8, count), f32),
        ],
        in_specs=[
            pl.BlockSpec((count, PAIR), lambda pair: (0, pair)),
            pl.BlockSpec((count, 128), lambda pair: (0, 0)),
            pl.BlockSpec((row_length, PAIR), lambda pair: (0, pair)),
            pl.BlockSpec((PAIR, row_length), lambda pair: (pair, 0)),
            pl.BlockSpec((row_length, 256), lambda pair: (0, pair)),
        ],
        out_specs=[
            pl.BlockSpec((PAIR, count), lambda pair: (pair, 0)),
            pl.BlockSpec((16, count), lambda pair: (pair, 0)),
        ],
        compiler_params=pltpu.CompilerParams(vmem_limit_bytes=vmem_bytes),
        cost_estimate=pl.CostEstimate(
            flops=4 * HEADS * count * row_length * 256,
            bytes_accessed=HEADS * row_length * 1024,
            transcendentals=HEADS * count * row_length,
        ),
        name="attention_forward",
    )(queries, extra, keys, values_t, keys_extra)


def backward_kernel(
    queries,
    query_rows,
    delta_rows,
    context_grad,
    queries_t,
    context_grad_t,
    keys,
    values_t,
    keys_extra,
    query_grad,
    key_grad_t,
    value_grad_t,
    folded,
):
    step = pl.program_id(1)
    count, amount = queries.shape[0], keys.shape[0]
    lane = lax.broadcasted_iota(jnp.int32, (count, PAIR), 1)
    query_pair, grad_pair = queries[...], context_grad[...]
    zeros = jnp.zeros_like(query_pair)

    @pl.when(step == 0)
    def _():
        query_grad[...] = jnp.zeros_like(query_grad)

    query_grads = []
    for head in range(2):
        mine = (lane < HEAD) if head == 0 else (lane >= HEAD)
        rows = pl.ds(HEAD * head, HEAD)
        more = keys_extra[:, 128 * head : 128 * head + 128]
        query_side = jnp.concatenate([jnp.where(mine, query_pair, zeros), query_rows[head]], axis=1)
        grad_side = jnp.concatenate([jnp.where(mine, grad_pair, zeros), delta_rows[head]], axis=1)
        key_side = jnp.concatenate([keys[...], more], axis=1)
        value_side = jnp.concatenate(
            [values_t[...], jnp.ones((128, amount), low_type)], axis=0
        )
        attention = jnp.exp(dot(query_side, key_side, 1, 1))
        score_grad = attention * dot(grad_side, value_side, 1, 0)
        attention_low = attention.astype(low_type)
        score_low = score_grad.astype(low_type)
        for block in range(count // BLK):
            folded[head, pl.ds(block, 1), :] = jnp.sum(
                score_grad[BLK * block : BLK * block + BLK], axis=0, keepdims=True
            )
        query_grads.append(dot(score_low, keys[...], 1, 0))
        value_grad_t[rows, :] = dot(context_grad_t[rows, :], attention_low, 1, 0).astype(low_type)
        key_grad_t[rows, :] = dot(queries_t[rows, :], score_low, 1, 0).astype(low_type)
    query_grad[...] += jnp.where(lane < HEAD, query_grads[0], query_grads[1])


def attend_back(
    queries, query_rows, delta_rows, context_grad, queries_t, context_grad_t, keys, values_t, keys_extra
):
    count, row_length = queries.shape[0], keys.shape[0]
    blocks = count // BLK
    of_pair = pl.BlockSpec((count, PAIR), lambda pair, step: (0, pair))
    of_pair_t = pl.BlockSpec((PAIR, count), lambda pair, step: (pair, 0))
    of_heads = pl.BlockSpec((2, count, 128), lambda pair, step: (pair, 0, 0))
    key_t = pl.BlockSpec((PAIR, back_step), lambda pair, step: (pair, step))
    return pl.pallas_call(
        backward_kernel,
        grid=(PAIRS, row_length // back_step),
        out_shape=[
            jax.ShapeDtypeStruct((count, D), f32),
            jax.ShapeDtypeStruct((D, row_length), low_type),
            jax.ShapeDtypeStruct((D, row_length), low_type),
            jax.ShapeDtypeStruct((HEADS, blocks, row_length), f32),
        ],
        in_specs=[
            of_pair,
            of_heads,
            of_heads,
            of_pair,
            of_pair_t,
            of_pair_t,
            pl.BlockSpec((back_step, PAIR), lambda pair, step: (step, pair)),
            key_t,
            pl.BlockSpec((back_step, 256), lambda pair, step: (step, pair)),
        ],
        out_specs=[
            of_pair,
            key_t,
            key_t,
            pl.BlockSpec((2, blocks, back_step), lambda pair, step: (pair, 0, step)),
        ],
        compiler_params=pltpu.CompilerParams(vmem_limit_bytes=vmem_bytes),
        cost_estimate=pl.CostEstimate(
            flops=10 * HEADS * count * row_length * 200,
            bytes_accessed=HEADS * row_length * 2048,
            transcendentals=HEADS * count * row_length,
        ),
        name="attention_backward",
    )(
        queries,
        query_rows,
        delta_rows,
        context_grad,
        queries_t,
        context_grad_t,
        keys,
        values_t,
        keys_extra,
    )


def body(
    hidden_states,
    output_cotangent,
    document_lengths,
    bucket_index,
    norm_gains,
    bias_table,
    project_weight,
    output_weight,
    expand_weight,
    reduce_weight,
    project_rows,
    project_columns,
    output_rows,
    output_columns,
    expand_rows,
    expand_columns,
    reduce_rows,
    reduce_columns,
    gains_moment,
    table_moment,
):
    every = ("seq", "dp")
    local_rows = hidden_states.shape[1]
    row_length = local_rows * lax.axis_size("seq")
    gradient_scale = 1.0 / math.sqrt(row_length * lax.axis_size("dp"))
    place = lax.axis_index("seq")
    blocks = local_rows // BLK

    project_full = lax.all_gather(project_weight.astype(low_type), every, axis=0, tiled=True)
    row_states = lax.all_gather(hidden_states[0], "seq", axis=0, tiled=True)
    mixed = jnp.concatenate([output_weight, expand_weight], axis=1).astype(low_type)
    mixed_full = lax.all_gather(mixed, every, axis=0, tiled=True)
    reduce_full = lax.all_gather(reduce_weight.astype(low_type), every, axis=0, tiled=True)
    output_full, expand_full = mixed_full[:, :D], mixed_full[:, D:]

    doc_all = documents(document_lengths[0], row_length)
    doc_query = lax.dynamic_slice_in_dim(doc_all, place * local_rows, local_rows)
    picks = key_picks(bucket_index[0], doc_all, bias_table.shape[0])
    keys_extra = key_extra(picks, bias_table, blocks)
    extra = query_extra(doc_query, blocks)

    inputs = hidden_states[0].astype(f32)
    normed_one, pullback_one = jax.vjp(rms_norm, inputs, norm_gains[0])
    normed_low = normed_one.astype(low_type)
    normed_all = rms_norm(row_states.astype(f32), norm_gains[0]).astype(low_type)
    query_weight, key_weight, value_weight = (
        project_full[:, :D],
        project_full[:, D : 2 * D],
        project_full[:, 2 * D :],
    )
    queries = (dot(normed_low, query_weight, 1, 0).astype(low_type).astype(f32) * score_scale).astype(
        low_type
    )
    queries_t = (
        dot(query_weight, normed_low, 0, 1).astype(low_type).astype(f32) * score_scale
    ).astype(low_type)
    keys = dot(normed_all, key_weight, 1, 0).astype(low_type)
    values_t = dot(value_weight, normed_all, 0, 1).astype(low_type)

    context_t, log_total = attend(queries, extra, keys, values_t, keys_extra)
    log_total = log_total.reshape(HEADS, 8, local_rows)[:, 0]
    context_low_t = context_t.astype(low_type)
    residual = inputs + dot(context_low_t, output_full, 0, 0)
    normed_two, pullback_two = jax.vjp(rms_norm, residual, norm_gains[1])
    normed_two_low = normed_two.astype(low_type)
    expanded = dot(normed_two_low, expand_full, 1, 0)
    activated, pullback_gelu = jax.vjp(gelu_tanh, expanded)
    activated_low = activated.astype(low_type)
    layer_output = (residual + dot(activated_low, reduce_full, 1, 0)).astype(low_type)[None]

    upstream_low = output_cotangent[0].astype(low_type)
    upstream = upstream_low.astype(f32)
    reduce_term = dot(activated_low, upstream_low, 0, 0)
    (expanded_grad,) = pullback_gelu(dot(upstream_low, reduce_full, 1, 1))
    expanded_low = expanded_grad.astype(low_type)
    expand_term = dot(normed_two_low, expanded_low, 0, 0)
    residual_part, gain_two_grad = pullback_two(dot(expanded_low, expand_full, 1, 1))
    residual_grad = upstream + residual_part
    residual_low = residual_grad.astype(low_type)
    output_term = dot(context_low_t, residual_low, 1, 0)
    context_grad = dot(residual_low, output_full, 1, 1).astype(low_type)
    context_grad_t = dot(output_full, residual_low, 1, 1).astype(low_type)
    delta = jnp.sum(
        (context_grad_t.astype(f32) * context_t).reshape(HEADS, HEAD, local_rows), axis=1
    )

    query_grad, key_grad_t, value_grad_t, folded = attend_back(
        queries,
        with_row_terms(extra, -log_total, blocks),
        with_row_terms(jnp.zeros_like(extra), -delta, blocks),
        context_grad,
        queries_t,
        context_grad_t,
        keys,
        values_t,
        keys_extra,
    )
    buckets = bias_table.shape[0]
    picked = jnp.dot(
        folded.reshape(HEADS * blocks, row_length),
        picks[:, : blocks * buckets].astype(f32),
        precision=lax.Precision.HIGHEST,
    )
    table_grad = jnp.einsum("hkkb->bh", picked.reshape(HEADS, blocks, blocks, buckets))

    query_grad_low = (query_grad * score_scale).astype(low_type)
    project_term = jnp.concatenate(
        [
            dot(normed_low, query_grad_low, 0, 0),
            dot(normed_all, key_grad_t, 0, 1),
            dot(normed_all, value_grad_t, 0, 1),
        ],
        axis=1,
    )
    key_part = dot(key_grad_t, key_weight, 0, 1) + dot(value_grad_t, value_weight, 0, 1)
    key_part = lax.psum_scatter(
        key_part.astype(low_type), "seq", scatter_dimension=0, tiled=True
    ).astype(f32)
    input_part, gain_one_grad = pullback_one(dot(query_grad_low, query_weight, 1, 1) + key_part)
    input_gradient = (residual_grad + input_part).astype(low_type)[None]

    mixed_term = jnp.concatenate([output_term, expand_term], axis=1).astype(low_type)
    scatter = lambda term: lax.psum_scatter(
        term.astype(low_type), every, scatter_dimension=0, tiled=True
    ).astype(f32)
    mixed_share = scatter(mixed_term)
    reduce_share = scatter(reduce_term)
    project_share = scatter(project_term)
    shares = (project_share, mixed_share[:, :D], mixed_share[:, D:], reduce_share)

    gradients = tuple((share * gradient_scale for share in shares))
    row_before = (project_rows, output_rows, expand_rows, reduce_rows)
    row_after = []
    column_parts = []
    row_sums = []
    for gradient, previous in zip(gradients, row_before):
        squares = gradient * gradient + tiny_term
        updated_rows = decay_rate * previous + (1.0 - decay_rate) * jnp.mean(squares, axis=1)
        row_after.append(updated_rows)
        column_parts.append(jnp.sum(squares, axis=0))
        row_sums.append(jnp.sum(updated_rows))
    summed = lax.psum(
        (
            column_parts[0],
            column_parts[1],
            column_parts[2],
            column_parts[3],
            jnp.stack(row_sums),
            jnp.stack([gain_one_grad, gain_two_grad]),
            table_grad,
        ),
        every,
    )
    column_before = (project_columns, output_columns, expand_columns, reduce_columns)
    weights_before = (project_weight, output_weight, expand_weight, reduce_weight)
    full_rows = (
        project_full.shape[0],
        output_full.shape[0],
        expand_full.shape[0],
        reduce_full.shape[0],
    )
    updated_weights = []
    columns_after = []
    for position in range(4):
        columns_new = decay_rate * column_before[position] + (1.0 - decay_rate) * (
            summed[position] / full_rows[position]
        )
        row_mean = summed[4][position] / full_rows[position]
        denominator = row_after[position][:, None] * columns_new[None, :] / row_mean
        updated_weights.append(
            weights_before[position] - learn_rate * gradients[position] * lax.rsqrt(denominator)
        )
        columns_after.append(columns_new)
    gains_gradient = summed[5] * gradient_scale
    table_gradient = summed[6] * gradient_scale
    gains_moment_new = decay_rate * gains_moment + (1.0 - decay_rate) * (
        gains_gradient * gains_gradient + tiny_term
    )
    gains_updated = norm_gains - learn_rate * gains_gradient * lax.rsqrt(gains_moment_new)
    table_moment_new = decay_rate * table_moment + (1.0 - decay_rate) * (
        table_gradient * table_gradient + tiny_term
    )
    table_updated = bias_table - learn_rate * table_gradient * lax.rsqrt(table_moment_new)
    return (
        layer_output,
        input_gradient,
        gains_gradient,
        table_gradient,
        gradients[0],
        gradients[1],
        gradients[2],
        gradients[3],
        gains_updated,
        table_updated,
        updated_weights[0],
        updated_weights[1],
        updated_weights[2],
        updated_weights[3],
        row_after[0],
        columns_after[0],
        row_after[1],
        columns_after[1],
        row_after[2],
        columns_after[2],
        row_after[3],
        columns_after[3],
        gains_moment_new,
        table_moment_new,
    )


def solution(mesh):
    placed = (
        P("dp", "seq", None),
        P("dp", "seq", None),
        P("dp", None),
        P("dp", "seq", None),
        P(),
        P(),
        P(("seq", "dp"), None),
        P(("seq", "dp"), None),
        P(("seq", "dp"), None),
        P(("seq", "dp"), None),
        P(("seq", "dp")),
        P(),
        P(("seq", "dp")),
        P(),
        P(("seq", "dp")),
        P(),
        P(("seq", "dp")),
        P(),
        P(),
        P(),
    )
    return jax.shard_map(
        body,
        mesh=mesh,
        in_specs=placed,
        out_specs=(
            P("dp", "seq", None),
            P("dp", "seq", None),
            P(),
            P(),
            P(("seq", "dp"), None),
            P(("seq", "dp"), None),
            P(("seq", "dp"), None),
            P(("seq", "dp"), None),
            P(),
            P(),
            P(("seq", "dp"), None),
            P(("seq", "dp"), None),
            P(("seq", "dp"), None),
            P(("seq", "dp"), None),
            P(("seq", "dp")),
            P(),
            P(("seq", "dp")),
            P(),
            P(("seq", "dp")),
            P(),
            P(("seq", "dp")),
            P(),
            P(),
            P(),
        ),
        check_vma=False,
    )
```

time: 2310 us -> 947 us (0.41)
  local copies, waits for them, and re-layouts: 786 us -> 33.2 us
  matrix products: 458 us -> 134 us
  waiting for transfers between devices: 823 us -> 530 us
  Pallas kernels: 0 us -> 120 us
  other arithmetic: 163 us -> 58.7 us
    add x96 -> x0, local copies, waits for them, and re-layouts: 410 us -> none  [block_scores(): (raw_scores * score_scale).reshape(heads_count, query_count // BLK, BLK,...]
    dot_general x252 -> x21, matrix products: 458 us -> 134 us  [the longest x20 129 us: dot(): lax.dot_general(former, latter, (((former_axis,), (latter_axis,)), ((), (...]
    reduce_scatter x5 -> x3, waiting for transfers between devices: 597 us -> 298 us  [the longest x2 221 us: body(): lax.psum_scatter(term.astype(low_type), every, scatter_dimension=0, tiled...]
    mul x24 -> x0, local copies, waits for them, and re-layouts: 145 us -> none  [back_block(): score_grad = attention * (attention_grad - delta_sum[:, :, None])]
    dynamic_slice x145 -> x1, local copies, waits for them, and re-layouts: 139 us -> 0.08 us  [body(): lax.dynamic_slice_in_dim(doc_all, place * local_rows, local_rows)]
    pallas_call x0 -> x2, Pallas kernels: none -> 120 us  [the longest x1 75.7 us: attend_back(): pl.pallas_call(backward_kernel, grid=(PAIRS, row_length // back_step), ou...]
    reduce_sum x48 -> x1, other arithmetic: 85.9 us -> 2.48 us  [body(): jnp.sum((context_grad_t.astype(f32) * context_t).reshape(HEADS, HEAD, loc...]
    while x264 -> x0, local copies, waits for them, and re-layouts: 49.5 us -> none
  transfers between devices with their start and end apart: 11 -> 8, of which waited for: 8 -> 8; matrix products, arithmetic and copies ran while one was open for 25% -> 14% of each run, Pallas kernels for 0% -> 5%
where the time goes in v1:
time: 947 us; the launch traced here: 937 us
  waiting for transfers between devices  530 us (56%)
  matrix products  134 us (14%)
  Pallas kernels  120 us (13%)
  other arithmetic  58.7 us (6%)
  blocking collectives  41.7 us (4%)
  local copies, waits for them, and re-layouts  33.2 us (4%)
  between operations  18.3 us (2%)
    reduce_scatter x2, waiting for transfers between devices, body(): lax.psum_scatter(term.astype(low_type), every, scatter_dimension=0, tiled...  221 us
    dot_general x20, matrix products, dot(): lax.dot_general(former, latter, (((former_axis,), (latter_axis,)), ((), (...  129 us
    all_gather x1, waiting for transfers between devices, body(): row_states = lax.all_gather(hidden_states[0], 'seq', axis=0, tiled=True)  85.8 us
    reduce_scatter x1, waiting for transfers between devices, body(): lax.psum_scatter(key_part.astype(low_type), 'seq', scatter_dimension=0, t...  76.5 us
    pallas_call x1, Pallas kernels, attend_back(): pl.pallas_call(backward_kernel, grid=(PAIRS, row_length // back_step), ou...  75.7 us
    all_gather x1, waiting for transfers between devices, body(): lax.all_gather(reduce_weight.astype(low_type), every, axis=0, tiled=True)  55.1 us
    all_gather x1, waiting for transfers between devices, body(): lax.all_gather(project_weight.astype(low_type), every, axis=0, tiled=True)  47.8 us
    pallas_call x1, Pallas kernels, attend(): pl.pallas_call(forward_kernel, grid=(PAIRS,), out_shape=[jax.ShapeDtypeSt...  44.8 us
  transfers between devices with their start and end apart: 8, of which 8 were waited for; matrix products, arithmetic and copies ran while one was open for 14% of the time, Pallas kernels for 5%

profile of v1, /device:TPU:0, one launch (start us, length us, event | category | flops | bytes accessed | tf_op | source)
XLA Modules:
  0.0 936.8 jit_solution(7870457769717607328)
XLA Ops:
  21.2 5.3 convolution_convert_fusion.keys_extra
  26.5 47.8 %all-gather.6.cloned.1.call-done = bf16[768,2304]{1,0:T(8,128)(2,1)} async-done(((bf16[24,2304]{1,0:T(8,128)(2,1)}), bf16[768,2304]{1,0:T(8,128)(2,1)}) %all-gather.6.cloned.1.call-update) | async-done | bytes 3538960 | tf_op jit(solution)/shard_map/all_gather | solution.py:319
  78.3 85.8 %all-gather.12.cloned.1.call-done = bf16[1,3072,768]{2,1,0:T(8,128)(2,1)} async-done(((bf16[1,768,768]{2,1,0:T(8,128)(2,1)}), bf16[1,3072,768]{2,1,0:T(8,128)(2,1)}) %all-gather.12.cloned.1.call-update) | async-done | bytes 4718608 | tf_op jit(solution)/shard_map/all_gather | solution.py:320
  164.1 3.5 fusion
  167.9 7.8 fusion.9.values_t
  175.7 7.5 convolution_convert_fusion.4.keys
  183.1 44.8 %attention_forward.1 = (f32[768,768]{1,0:T(8,128)}, f32[96,768]{1,0:T(8,128)}) custom-call(bf16[768,768]{1,0:T(8,128)(2,1)} %copy.111.queries, bf16[768,128]{1,0:T(8,128)(2,1)} %fusion.100.extra, bf16[3072,768]{1,0:T(8,128)(2,1)} %convolution_convert_fusion.4.keys, bf16[768,3072]{1,0:T(8,128)(2,1)} %fusion.9.values_t, ...), custom_call_target="tpu_custom_call" | custom-call | flops 28991029248 | bytes 37748736 | tf_op jit(solution)/shard_map/attention_forward/pallas_call | solution.py:157
  229.5 4.8 all-gather.8.cloned.1.call-done
  238.1 6.6 fusion.12
  244.6 55.1 %all-gather.10.cloned.1.call-done = bf16[3072,768]{1,0:T(8,128)(2,1)} async-done(((bf16[96,768]{1,0:T(8,128)(2,1)}), bf16[3072,768]{1,0:T(8,128)(2,1)}) %all-gather.10.cloned.1.call-update) | async-done | bytes 4718608 | tf_op jit(solution)/shard_map/all_gather | solution.py:323
  299.7 13.9 %fusion.6 = bf16[768,3072]{1,0:T(8,128)(2,1)S(1)} fusion(f32[768,3072]{1,0:T(8,128)} %fusion.12, bf16[3072,768]{1,0:T(8,128)(2,1)} %all-gather.10.cloned.1.call-done, bf16[1,768,768]{2,1,0:T(8,128)(2,1)} %param.21), kind=kOutput, calls=%fused_computation.14 | convolution fusion | flops 3680501760 | bytes 20054016 | tf_op jit(solution)/shard_map/dot_general | solution.py:33
  313.7 8.5 multiply_reduce_fusion
  324.7 4.1 convert_multiply_fusion.6
  332.1 11.3 %select_convert_fusion = (bf16[12,768,128]{2,1,0:T(8,128)(2,1)}, bf16[12,768,128]{2,1,0:T(8,128)(2,1)}) fusion(bf16[12,768]{1,0:T(8,128)(2,1)S(1)} %get-tuple-element.174, bf16[12,768]{1,0:T(8,128)(2,1)S(1)} %get-tuple-element.173, bf16[12,768]{1,0:T(8,128)(2,1)S(1)} %get-tuple-element.172, pred[128]{0:T(512)(128)(4,1)} %get-tuple-element.201, ...), kind=kLoop, calls=%fused_computation.29 | loop fusion | flops 7077888 | bytes 5026176 | tf_op jit(solution)/shard_map/convert_element_type | solution.py:93
  343.4 3.4 convolution_convert_fusion.9.context_grad
  346.9 75.7 %attention_backward.1 = (f32[768,768]{1,0:T(8,128)}, bf16[768,3072]{1,0:T(8,128)(2,1)}, bf16[768,3072]{1,0:T(8,128)(2,1)}, f32[12,6,3072]{2,1,0:T(8,128)}) custom-call(bf16[768,768]{1,0:T(8,128)(2,1)} %copy.111.queries, bf16[12,768,128]{2,1,0:T(8,128)(2,1)} %get-tuple-element.184.query_rows, bf16[12,768,128]{2,1,0:T(8,128)(2,1)} %get-tuple-element.183.delta_rows, ...), custom_call_target="tpu_custom_call" | custom-call | flops 56623104000 | bytes 75497472 | tf_op jit(solution)/shard_map/attention_backward/pallas_call | solution.py:244
  428.7 7.9 convolution_convert_fusion.6
  436.6 4.1 convolution_convert_fusion.5
  442.7 5.8 copy.136
  448.6 9.9 %convolution_convert_fusion.1 = bf16[3072,768]{1,0:T(8,128)(2,1)} fusion(bf16[1,768,768]{2,1,0:T(8,128)(2,1)} %param.21, f32[768,3072]{1,0:T(8,128)} %fusion.12), kind=kOutput, calls=%fused_computation.20 | convolution fusion | flops 3647471616 | bytes 15335424 | tf_op jit(solution)/shard_map/dot_general | solution.py:33
  458.5 3.9 convolution_convert_fusion.7
  464.8 7.2 convolution_convert_fusion.2
  475.0 6.3 fusion.50
  481.3 8.9 add_convert_fusion
  492.6 11.3 %fusion.27 = bf16[1,768,768]{1,2,0:T(8,128)(2,1)} fusion(f32[768,768]{0,1:T(8,128)} %copy-done, bf16[3072,768]{1,0:T(8,128)(2,1)} %all-gather.10.cloned.1.call-done, f32[768,3072]{1,0:T(8,128)} %fusion.12), kind=kOutput, calls=%fused_computation.71 | convolution fusion | flops 3646291968 | bytes 17694720 | tf_op jit(solution)/shard_map/dot_general | solution.py:33
  507.2 5.4 fusion.43
  512.6 37.8 %reduce-scatter.13.cloned.1.call-done = bf16[24,2304]{1,0:T(8,128)(2,1)} async-done(((bf16[768,2304]{1,0:T(8,128)(2,1)}), bf16[24,2304]{1,0:T(8,128)(2,1)}) %reduce-scatter.13.cloned.1.call-update) | async-done | bytes 110608
  554.9 106.7 %reduce-scatter.11.cloned.1.call-done = bf16[96,768]{1,0:T(8,128)(2,1)} async-done(((bf16[3072,768]{1,0:T(8,128)(2,1)}), bf16[96,768]{1,0:T(8,128)(2,1)}) %reduce-scatter.11.cloned.1.call-update) | async-done | bytes 147472 | tf_op jit(solution)/shard_map/reduce_scatter | solution.py:413
  665.6 114.4 %reduce-scatter.9.cloned.1.call-done = bf16[24,3840]{1,0:T(8,128)(2,1)} async-done(((bf16[768,3840]{1,0:T(8,128)(2,1)}), bf16[24,3840]{1,0:T(8,128)(2,1)}) %reduce-scatter.9.cloned.1.call-update) | async-done | bytes 184336 | tf_op jit(solution)/shard_map/reduce_scatter | solution.py:413
  790.4 76.5 %reduce-scatter.7.cloned.1.call-done = bf16[768,768]{0,1:T(8,128)(2,1)} async-done(((bf16[3072,768]{0,1:T(8,128)(2,1)}), bf16[768,768]{0,1:T(8,128)(2,1)}) %reduce-scatter.7.cloned.1.call-update) | async-done | bytes 1179664 | tf_op jit(solution)/shard_map/reduce_scatter | solution.py:406
  866.9 3.8 fusion.21
  875.7 41.7 %all-reduce = (f32[2,768]{1,0:T(2,128)S(1)}, f32[32,12]{0,1:T(8,128)S(1)}, f32[4]{0:T(128)S(1)}, f32[2304]{0:T(1024)S(1)}, f32[768]{0:T(1024)S(1)}, /*index=5*/f32[3072]{0:T(1024)S(1)}, f32[768]{0:T(1024)S(1)}) all-reduce(f32[2,768]{1,0:T(2,128)S(1)} %pad_maximum_fusion.4, ...), channel_id=1, replica_groups=mesh['seq'=4,'dp'=8] {'seq','dp'}, use_global_device_ids=true, to_apply=%region_11.12 | all-reduce | flops 8836 | bytes 70688 | tf_op jit(solution)/shard_map/psum | solution.py:432
  (241 shorter events, 81.3 us)
Async XLA Ops:
  7.2 7.2 copy-start.5
  7.2 67.1 %all-gather.6.cloned.1.call-start = ((), (), s32[]{:S(2)}) async-start(), calls=%async_computation.4 | async-start | bytes 3649536 | tf_op jit(solution)/shard_map/all_gather | solution.py:319
  9.0 6.4 copy-start.26
  9.0 155.1 %all-gather.12.cloned.1.call-start = ((), (), s32[]{:S(2)}) async-start(), calls=%async_computation.10 | async-start | bytes 5898240 | tf_op jit(solution)/shard_map/all_gather | solution.py:320
  9.8 224.5 %all-gather.8.cloned.1.call-start = ((), (), s32[]{:S(2)}) async-start(), calls=%async_computation.5 | async-start | bytes 6082560 | tf_op jit(solution)/shard_map/all_gather | solution.py:322
  12.4 287.3 %all-gather.10.cloned.1.call-start = ((), (), s32[]{:S(2)}) async-start(), calls=%async_computation.6 | async-start | bytes 4866048 | tf_op jit(solution)/shard_map/all_gather | solution.py:323
  13.2 537.1 %reduce-scatter.13.cloned.1.call-start = ((), (), s32[]{:S(2)}) async-start(), calls=%async_computation.11 | async-start | bytes 3649536
  15.4 421.2 %copy-start.28 = (f32[768]{0:T(1024)}, f32[768]{0:T(1024)S(1)}, u32[]{:S(2)}) copy-start(f32[768]{0:T(1024)S(1)} %get-tuple-element.145) | copy-start | bytes 9220
  17.2 57.1 %copy-start.33 = (f32[768]{0:T(1024)}, f32[768]{0:T(1024)S(1)}, u32[]{:S(2)}) copy-start(f32[768]{0:T(1024)S(1)} %fusion.88) | copy-start | bytes 9220
  76.8 90.8 %copy-start.12 = (bf16[768,768]{0,1:T(8,128)(2,1)}, bf16[768,768]{0,1:T(8,128)(2,1)S(1)}, u32[]{:S(2)}) copy-start(bf16[768,768]{0,1:T(8,128)(2,1)S(1)} %multiply_convert_fusion.3) | copy-start | bytes 3538948
  167.9 7.8 copy-start.37
  237.6 76.0 %copy-start = (f32[768,768]{0,1:T(8,128)}, f32[768,768]{0,1:T(8,128)S(1)}, u32[]{:S(2)}) copy-start(f32[768,768]{0,1:T(8,128)S(1)} %get-tuple-element.190) | copy-start | bytes 7077892
  313.6 8.5 copy-start.57
  313.7 8.5 copy-start.3
  425.6 10.9 %slice-start.2 = ((s8[4718592]{0:T(1024)(128)(4,1)}), s8[4194304]{0:T(1024)(128)(4,1)S(1)}, s32[]{:S(2)}) async-start(s8[4718592]{0:T(1024)(128)(4,1)} %bitcast.124), calls=%async_computation.14 | async-start | bytes 8388608
  425.6 10.9 %slice-start.4 = ((s8[4718592]{0:T(1024)(128)(4,1)}), s8[4194304]{0:T(1024)(128)(4,1)S(1)}, s32[]{:S(2)}) async-start(s8[4718592]{0:T(1024)(128)(4,1)} %bitcast.137), calls=%async_computation.16 | async-start | bytes 8388608
  428.7 7.9 slice-start.3
  428.7 7.9 slice-start.5
  448.5 213.1 %reduce-scatter.11.cloned.1.call-start = ((), (), s32[]{:S(2)}) async-start(), calls=%async_computation.9 | async-start | bytes 4866048 | tf_op jit(solution)/shard_map/reduce_scatter | solution.py:413
  458.5 321.6 %reduce-scatter.9.cloned.1.call-start = ((), (), s32[]{:S(2)}) async-start(), calls=%async_computation.8 | async-start | bytes 6082560 | tf_op jit(solution)/shard_map/reduce_scatter | solution.py:413
  464.8 7.2 copy-start.4
  474.9 392.0 %reduce-scatter.7.cloned.1.call-start = ((), (), s32[]{:S(2)}) async-start(), calls=%async_computation.7 | async-start | bytes 5898240 | tf_op jit(solution)/shard_map/reduce_scatter | solution.py:406
  507.2 46.6 %copy-start.55 = (f32[24]{0:T(128)S(1)}, f32[24]{0:T(128)}, u32[]{:S(2)}) copy-start(f32[24]{0:T(128)} %param.30) | copy-start | bytes 292
  790.4 81.0 %copy-start.23 = (f32[768]{0:T(1024)S(1)}, f32[768]{0:T(1024)}, u32[]{:S(2)}) copy-start(f32[768]{0:T(1024)} %copy-done.22) | copy-start | bytes 9220
  873.1 46.9 %copy-start.41 = (f32[2304]{0:T(1024)S(1)}, f32[2304]{0:T(1024)}, u32[]{:S(2)}) copy-start(f32[2304]{0:T(1024)} %param.31) | copy-start | bytes 27652
  873.1 46.9 %copy-start.2 = (bf16[24,2304]{0,1:T(8,128)(2,1)S(1)}, bf16[24,2304]{0,1:T(8,128)(2,1)}, u32[]{:S(2)}) copy-start(bf16[24,2304]{0,1:T(8,128)(2,1)} %copy.137) | copy-start | bytes 331780
  873.1 46.9 %copy-start.7 = (f32[24,2304]{0,1:T(8,128)S(1)}, f32[24,2304]{0,1:T(8,128)}, u32[]{:S(2)}) copy-start(f32[24,2304]{0,1:T(8,128)} %copy.123) | copy-start | bytes 663556
  873.1 46.9 %copy-start.53 = (f32[24]{0:T(128)S(1)}, f32[24]{0:T(128)}, u32[]{:S(2)}) copy-start(f32[24]{0:T(128)} %get-tuple-element.160) | copy-start | bytes 292
  921.5 6.3 copy-start.15
  921.5 7.1 copy-start.14
  921.5 7.1 copy-start.16
  921.6 7.1 copy-start.52
  (40 other events, 156.2 us)
Sparse Core Ops, SparseCore 0:
  11.5 62.7 all-gather.5
  75.9 88.1 all-gather.11
  167.6 66.6 all-gather.7
  237.6 62.1 all-gather.9
  448.7 101.6 reduce-scatter.12
  555.7 105.8 reduce-scatter.10
  668.2 111.7 reduce-scatter.8
  782.4 84.4 reduce-scatter.6

commit v2 on v1

--- a/solution.py
+++ b/solution.py
@@ -1,3 +1,4 @@
+import functools
 import math
 
 import jax
@@ -287,6 +288,350 @@
     )
 
 
+MESH = pl.DeviceIdType.MESH
+
+
+class Place:
+    def __init__(self):
+        self.seq, self.dp = lax.axis_index("seq"), lax.axis_index("dp")
+        self.core, self.x, self.y = self.dp % 2, self.dp // 2 % 2, self.dp // 4
+        self.by_core = (self.seq, self.dp + 1 - 2 * self.core)
+        self.by_x = (self.seq, self.dp + 2 - 4 * self.x)
+        self.by_y = (self.seq, self.dp + 4 - 8 * self.y)
+        self.others = [((self.seq + step) % 4, self.dp) for step in (1, 2, 3)]
+
+    def greet(self):
+        barrier = pltpu.get_barrier_semaphore()
+        partners = [self.by_core, self.by_x, self.by_y] + self.others
+        for partner in partners:
+            pl.semaphore_signal(barrier, inc=1, device_id=partner, device_id_type=MESH)
+        pl.semaphore_wait(barrier, len(partners))
+
+
+def send(source, target, sems, index, partner):
+    return pltpu.make_async_remote_copy(
+        src_ref=source,
+        dst_ref=target,
+        send_sem=sems.at[0, index],
+        recv_sem=sems.at[1, index],
+        device_id=partner,
+        device_id_type=MESH,
+    )
+
+
+def half_of(width, which):
+    return pl.ds(pl.multiple_of(which * (width // 2), 128), width // 2)
+
+
+class Gather:
+    steps = 6
+
+    def __init__(self, at, shard, pair, low, whole, sems, local_sems, x_first):
+        self.at, self.shard, self.pair, self.low, self.whole = at, shard, pair, low, whole
+        rows, width = shard.shape
+        mine, other = half_of(width, at.core), half_of(width, 1 - at.core)
+        own_rows = pl.ds(pl.multiple_of(rows * at.core, 8), rows)
+        place = whole.at[at.seq, at.y, at.x, :, mine]
+        along_x, along_y = (whole.at[:, at.y, at.x, :, mine], whole.at[:, at.y, :, :, mine])
+        if not x_first:
+            along_x, along_y = (whole.at[:, :, at.x, :, mine], along_x)
+        self.local = [
+            pltpu.make_async_copy(shard.at[:, mine], pair.at[own_rows], local_sems.at[0]),
+            pltpu.make_async_copy(low, place, local_sems.at[1]),
+        ]
+        self.first = send(shard.at[:, other], pair.at[own_rows], sems, 0, at.by_core)
+        self.over_z = [send(low, place, sems, 1 + k, at.others[k]) for k in range(3)]
+        self.over_x = send(along_x, along_x, sems, 4, at.by_x)
+        self.over_y = send(along_y, along_y, sems, 5, at.by_y)
+        self.order = [self.over_x, self.over_y] if x_first else [self.over_y, self.over_x]
+        self.last = send(whole.at[:, :, :, :, mine], whole.at[:, :, :, :, mine], sems, 6, at.by_core)
+
+    def step(self, number):
+        if number == 0:
+            self.local[0].start()
+            self.first.start()
+        elif number == 1:
+            self.local[0].wait()
+            self.first.wait()
+            self.low[...] = self.pair[...].astype(low_type)
+            self.local[1].start()
+            for copy in self.over_z:
+                copy.start()
+        elif number == 2:
+            self.local[1].wait()
+            for copy in self.over_z:
+                copy.wait()
+            self.order[0].start()
+        elif number == 3:
+            self.order[0].wait()
+            self.order[1].start()
+        elif number == 4:
+            self.order[1].wait()
+            self.last.start()
+        else:
+            self.last.wait()
+
+
+class Scatter:
+    steps = 6
+
+    def __init__(self, at, term, held, arrived, total, share, sems, local_sems, x_first):
+        self.at, self.held, self.arrived, self.total = at, held, arrived, total
+        self.x_first = x_first
+        width = term.shape[4]
+        rows = term.shape[3] // 2
+        mine, other = half_of(width, at.core), half_of(width, 1 - at.core)
+        of_core = lambda which: pl.ds(pl.multiple_of(rows * which, 8), rows)
+        self.local = [
+            pltpu.make_async_copy(term.at[:, :, :, :, mine], held, local_sems.at[0]),
+            pltpu.make_async_copy(total.at[of_core(at.core)], share.at[:, mine], local_sems.at[1]),
+        ]
+        self.first = send(term.at[:, :, :, :, other], arrived[0], sems, 0, at.by_core)
+        if x_first:
+            self.second = send(held.at[:, :, 1 - at.x], arrived[1], sems, 1, at.by_x)
+            self.third = send(held.at[:, 1 - at.y, at.x], arrived[2], sems, 2, at.by_y)
+        else:
+            self.second = send(held.at[:, 1 - at.y], arrived[1], sems, 1, at.by_y)
+            self.third = send(held.at[:, at.y, 1 - at.x], arrived[2], sems, 2, at.by_x)
+        self.over_z = [
+            send(held.at[at.others[k][0], at.y, at.x], arrived[3].at[k], sems, 3 + k, at.others[k])
+            for k in range(3)
+        ]
+        self.last = send(total.at[of_core(1 - at.core)], share.at[:, mine], sems, 6, at.by_core)
+
+    def add(self, place, values):
+        self.held[place] = (self.held[place].astype(f32) + values.astype(f32)).astype(low_type)
+
+    def step(self, number):
+        at = self.at
+        if number == 0:
+            self.local[0].start()
+            self.first.start()
+        elif number == 1:
+            self.local[0].wait()
+            self.first.wait()
+
+            @pl.loop(0, 4)
+            def _(row):
+                for across in range(4):
+                    place = (row, across // 2, across % 2)
+                    self.add(place, self.arrived[0][place])
+
+            self.second.start()
+        elif number == 2:
+            self.second.wait()
+
+            @pl.loop(0, 4)
+            def _(row):
+                for across in range(2):
+                    place = (row, across, at.x) if self.x_first else (row, at.y, across)
+                    self.add(place, self.arrived[1][row, across])
+
+            self.third.start()
+        elif number == 3:
+            self.third.wait()
+
+            @pl.loop(0, 4)
+            def _(row):
+                self.add((row, at.y, at.x), self.arrived[2][row])
+
+            for copy in self.over_z:
+                copy.start()
+        elif number == 4:
+            for copy in self.over_z:
+                copy.wait()
+            total = self.held[at.seq, at.y, at.x].astype(f32)
+            for k in range(3):
+                total = total + self.arrived[3][k].astype(f32)
+            self.total[...] = total
+            self.local[1].start()
+            self.last.start()
+        else:
+            self.local[1].wait()
+            self.last.wait()
+
+
+class Ring:
+    def __init__(self, at, own, blocks, sems, local_sem):
+        self.at = at
+        seq = at.seq
+        self.local = pltpu.make_async_copy(own, blocks.at[seq], local_sem)
+        right, left = ((seq + 1) % 4, at.dp), ((seq + 3) % 4, at.dp)
+        self.hops = []
+        for hop in range(3):
+            back, ahead = (seq + 4 - hop) % 4, (seq + hop) % 4
+            block_back = own if hop == 0 else blocks.at[back]
+            block_ahead = own if hop == 0 else blocks.at[ahead]
+            self.hops.append(
+                [
+                    (
+                        (seq >= hop) & (seq < 3),
+                        send(block_back, blocks.at[back], sems, hop, right),
+                        seq >= hop + 1,
+                    ),
+                    (
+                        (seq + hop <= 3) & (seq > 0),
+                        send(block_ahead, blocks.at[ahead], sems, 3 + hop, left),
+                        seq + hop + 1 <= 3,
+                    ),
+                ]
+            )
+
+    def start(self, hop):
+        if hop == 0:
+            self.local.start()
+        for sends, copy, _ in self.hops[hop]:
+            pl.when(sends)(copy.start)
+
+    def arrive(self, hop):
+        for _, copy, receives in self.hops[hop]:
+            pl.when(receives)(copy.wait_recv)
+
+    def finish(self):
+        self.local.wait()
+        for hop in self.hops:
+            for sends, copy, _ in hop:
+                pl.when(sends)(copy.wait_send)
+
+
+X_FIRST = (True, False, False, True)
+
+
+def remote_scratch(shapes):
+    return [pltpu.SemaphoreType.DMA((2, 7)), pltpu.SemaphoreType.DMA((2,))] * len(shapes)
+
+
+def gather_kernel(*refs):
+    shards, own, wholes, blocks = refs[:4], refs[4], refs[5:9], refs[9]
+    scratch = refs[10:]
+    pairs, lows, sems = scratch[:4], scratch[4:8], scratch[8:16]
+    ring_sems, ring_local = scratch[16:]
+    at = Place()
+    at.greet()
+    gathers = [
+        Gather(
+            at,
+            shards[k],
+            pairs[k],
+            lows[k],
+            wholes[k],
+            sems[2 * k],
+            sems[2 * k + 1],
+            X_FIRST[k],
+        )
+        for k in range(4)
+    ]
+    ring = Ring(at, own, blocks, ring_sems, ring_local.at[0])
+    for gather in gathers:
+        gather.step(0)
+    gathers[0].step(1)
+    ring.start(0)
+    for number in range(2, 4):
+        gathers[0].step(number)
+    for gather in gathers[1:]:
+        gather.step(1)
+    ring.arrive(0)
+    ring.start(1)
+    for number in range(4, 6):
+        gathers[0].step(number)
+    for gather in gathers[1:]:
+        gather.step(2)
+    ring.arrive(1)
+    ring.start(2)
+    for number in range(3, 6):
+        for gather in gathers[1:]:
+            gather.step(number)
+    ring.arrive(2)
+    ring.finish()
+
+
+def gather_weights(shards, own):
+    low_shape = lambda shard: (2 * shard.shape[0], shard.shape[1] // 2)
+    anywhere = pl.BlockSpec(memory_space=pl.ANY)
+    return pl.pallas_call(
+        gather_kernel,
+        out_shape=[
+            jax.ShapeDtypeStruct((4, 2, 2, 2 * shard.shape[0], shard.shape[1]), low_type)
+            for shard in shards
+        ]
+        + [jax.ShapeDtypeStruct((4,) + own.shape, low_type)],
+        in_specs=[anywhere] * 5,
+        out_specs=[anywhere] * 5,
+        scratch_shapes=[pltpu.VMEM(low_shape(shard), f32) for shard in shards]
+        + [pltpu.VMEM(low_shape(shard), low_type) for shard in shards]
+        + remote_scratch(shards)
+        + [pltpu.SemaphoreType.DMA((2, 6)), pltpu.SemaphoreType.DMA((1,))],
+        compiler_params=pltpu.CompilerParams(
+            collective_id=0, has_side_effects=True, vmem_limit_bytes=vmem_bytes
+        ),
+        name="gather_weights",
+    )(*shards, own)
+
+
+def scatter_kernel(count, *refs):
+    terms, shares, scratch = refs[:count], refs[count : 2 * count], refs[2 * count :]
+    held, arrived, totals, sems = (
+        scratch[:count],
+        scratch[count : 5 * count],
+        scratch[5 * count : 6 * count],
+        scratch[6 * count :],
+    )
+    at = Place()
+    at.greet()
+    scatters = [
+        Scatter(
+            at,
+            terms[k],
+            held[k],
+            arrived[4 * k : 4 * k + 4],
+            totals[k],
+            shares[k],
+            sems[2 * k],
+            sems[2 * k + 1],
+            k % 2 == 0,
+        )
+        for k in range(count)
+    ]
+    for number in range(Scatter.steps):
+        for scatter in scatters:
+            scatter.step(number)
+
+
+def scatter_scratch(terms, x_firsts):
+    held, arrived, totals = [], [], []
+    for term, x_first in zip(terms, x_firsts):
+        rows, half = term.shape[3], term.shape[4] // 2
+        held.append(pltpu.VMEM((4, 2, 2, rows, half), low_type))
+        arrived += [
+            pltpu.VMEM((4, 2, 2, rows, half), low_type),
+            pltpu.VMEM((4, 2, rows, half), low_type),
+            pltpu.VMEM((4, rows, half), low_type),
+            pltpu.VMEM((3, rows, half), low_type),
+        ]
+        totals.append(pltpu.VMEM((rows, half), f32))
+    return held + arrived + totals + remote_scratch(terms)
+
+
+def scatter_terms(terms, number):
+    terms = [
+        term.reshape(4, 2, 2, term.shape[0] // 16, term.shape[1]) for term in terms
+    ]
+    anywhere = pl.BlockSpec(memory_space=pl.ANY)
+    return pl.pallas_call(
+        functools.partial(scatter_kernel, len(terms)),
+        out_shape=[
+            jax.ShapeDtypeStruct((term.shape[3] // 2, term.shape[4]), f32) for term in terms
+        ],
+        in_specs=[anywhere] * len(terms),
+        out_specs=[anywhere] * len(terms),
+        scratch_shapes=scatter_scratch(terms, [k % 2 == 0 for k in range(len(terms))]),
+        compiler_params=pltpu.CompilerParams(
+            collective_id=number, has_side_effects=True, vmem_limit_bytes=vmem_bytes
+        ),
+        name="scatter_terms",
+    )(*terms)
+
+
 def body(
     hidden_states,
     output_cotangent,
@@ -316,12 +661,23 @@
     place = lax.axis_index("seq")
     blocks = local_rows // BLK
 
-    project_full = lax.all_gather(project_weight.astype(low_type), every, axis=0, tiled=True)
-    row_states = lax.all_gather(hidden_states[0], "seq", axis=0, tiled=True)
-    mixed = jnp.concatenate([output_weight, expand_weight], axis=1).astype(low_type)
-    mixed_full = lax.all_gather(mixed, every, axis=0, tiled=True)
-    reduce_full = lax.all_gather(reduce_weight.astype(low_type), every, axis=0, tiled=True)
-    output_full, expand_full = mixed_full[:, :D], mixed_full[:, D:]
+    shards = (project_weight, output_weight, expand_weight, reduce_weight)
+    direct = (
+        lax.axis_size("seq") == 4
+        and lax.axis_size("dp") == 8
+        and all(shard.shape[0] % 8 == 0 and shard.shape[1] % 256 == 0 for shard in shards)
+    )
+    if direct:
+        *wholes, row_states = gather_weights(shards, hidden_states[0])
+        project_full, output_full, expand_full, reduce_full = (
+            whole.reshape(-1, whole.shape[4]) for whole in wholes
+        )
+        row_states = row_states.reshape(row_length, -1)
+    else:
+        project_full, output_full, expand_full, reduce_full = (
+            lax.all_gather(shard.astype(low_type), every, axis=0, tiled=True) for shard in shards
+        )
+        row_states = lax.all_gather(hidden_states[0], "seq", axis=0, tiled=True)
 
     doc_all = documents(document_lengths[0], row_length)
     doc_query = lax.dynamic_slice_in_dim(doc_all, place * local_rows, local_rows)
@@ -409,14 +765,16 @@
     input_part, gain_one_grad = pullback_one(dot(query_grad_low, query_weight, 1, 1) + key_part)
     input_gradient = (residual_grad + input_part).astype(low_type)[None]
 
-    mixed_term = jnp.concatenate([output_term, expand_term], axis=1).astype(low_type)
-    scatter = lambda term: lax.psum_scatter(
-        term.astype(low_type), every, scatter_dimension=0, tiled=True
-    ).astype(f32)
-    mixed_share = scatter(mixed_term)
-    reduce_share = scatter(reduce_term)
-    project_share = scatter(project_term)
-    shares = (project_share, mixed_share[:, :D], mixed_share[:, D:], reduce_share)
+    terms = [
+        term.astype(low_type) for term in (project_term, output_term, expand_term, reduce_term)
+    ]
+    if direct:
+        shares = scatter_terms(terms, 1)
+    else:
+        shares = [
+            lax.psum_scatter(term, every, scatter_dimension=0, tiled=True).astype(f32)
+            for term in terms
+        ]
 
     gradients = tuple((share * gradient_scale for share in shares))
     row_before = (project_rows, output_rows, expand_rows, reduce_rows)

time: 947 us -> 628 us (0.66)
  waiting for transfers between devices: 530 us -> 45.6 us
  Pallas kernels: 120 us -> 345 us
  local copies, waits for them, and re-layouts: 33.2 us -> 14.3 us
  matrix products: 134 us -> 116 us
  other arithmetic: 58.7 us -> 42.7 us
    pallas_call x0 -> x2, Pallas kernels: none -> 224 us  [the longest x1 130 us: gather_weights(): pl.pallas_call(gather_kernel, out_shape=[jax.ShapeDtypeStruct((4, 2, 2, 2...]
    reduce_scatter x2 -> x0, waiting for transfers between devices: 221 us -> none  [body(): lax.psum_scatter(term.astype(low_type), every, scatter_dimension=0, tiled...]
    all_gather x4 -> x0, waiting for transfers between devices: 194 us -> none  [the longest x1 85.8 us: body(): row_states = lax.all_gather(hidden_states[0], 'seq', axis=0, tiled=True)]
    unnamed x9 -> x1, waiting for transfers between devices: 38.6 us -> 0.02 us
    reduce_scatter x1, waiting for transfers between devices: 76.5 us -> 45.6 us  [body(): lax.psum_scatter(key_part.astype(low_type), 'seq', scatter_dimension=0, t...]
    unnamed x140 -> x149, local copies, waits for them, and re-layouts: 21.9 us -> 1.79 us
    dot_general x20 -> x21, matrix products: 129 us -> 110 us  [dot(): lax.dot_general(former, latter, (((former_axis,), (latter_axis,)), ((), (...]
  transfers between devices with their start and end apart: 8 -> 1, of which waited for: 8 -> 1; matrix products, arithmetic and copies ran while one was open for 14% -> 8% of each run, Pallas kernels for 5% -> 0%
where the time goes in v2:
time: 628 us; the launch traced here: 622 us
  Pallas kernels  345 us (55%)
  matrix products  116 us (18%)
  waiting for transfers between devices  45.6 us (7%)
  other arithmetic  42.7 us (7%)
  blocking collectives  41.3 us (7%)
  between operations  18 us (3%)
  local copies, waits for them, and re-layouts  14.3 us (2%)
    pallas_call x1, Pallas kernels, gather_weights(): pl.pallas_call(gather_kernel, out_shape=[jax.ShapeDtypeStruct((4, 2, 2, 2...  130 us
    dot_general x21, matrix products, dot(): lax.dot_general(former, latter, (((former_axis,), (latter_axis,)), ((), (...  110 us
    pallas_call x1, Pallas kernels, scatter_terms(): pl.pallas_call(functools.partial(scatter_kernel, len(terms)), out_shape=[...  94.3 us
    pallas_call x1, Pallas kernels, attend_back(): pl.pallas_call(backward_kernel, grid=(PAIRS, row_length // back_step), ou...  75.7 us
    reduce_scatter x1, waiting for transfers between devices, body(): lax.psum_scatter(key_part.astype(low_type), 'seq', scatter_dimension=0, t...  45.6 us
    pallas_call x1, Pallas kernels, attend(): pl.pallas_call(forward_kernel, grid=(PAIRS,), out_shape=[jax.ShapeDtypeSt...  44.8 us
    psum x1, blocking collectives, body(): lax.psum((column_parts[0], column_parts[1], column_parts[2], column_parts...  41.3 us
  transfers between devices with their start and end apart: 1, of which 1 were waited for; matrix products, arithmetic and copies ran while one was open for 8% of the time, Pallas kernels for 0%

profile of v2, /device:TPU:0, one launch (start us, length us, event | category | flops | bytes accessed | tf_op | source)
XLA Modules:
  0.0 622.5 jit_solution(18242586284408009503)
XLA Ops:
  10.5 130.0 %gather_weights.1 = (bf16[4,2,2,48,2304]{4,3,2,1,0:T(8,128)(2,1)}, bf16[4,2,2,48,768]{4,3,2,1,0:T(8,128)(2,1)}, bf16[4,2,2,48,3072]{4,3,2,1,0:T(8,128)(2,1)}, bf...) custom-call(f32[24,2304]{1,0:T(8,128)} %refs_0_.1, f32[24,768]{1,0:T(8,128)} %refs_1_.1, f32[24,3072]{1,0:T(8,128)} %refs_2_.1, ...), custom_call_target="tpu_custom_call" | custom-call | tf_op jit(solution)/shard_map/gather_weights/pallas_call | solution.py:551
  140.5 3.4 multiply_convert_fusion.4.queries
  143.9 3.7 multiply_convert_fusion.2.queries_t
  148.7 3.6 fusion.10
  152.3 5.7 convolution_convert_fusion.3.values_t
  158.0 5.5 convolution_convert_fusion.4.keys
  166.3 5.3 convolution_convert_fusion.keys_extra
  173.0 44.8 %attention_forward.1 = (f32[768,768]{1,0:T(8,128)}, f32[96,768]{1,0:T(8,128)}) custom-call(bf16[768,768]{1,0:T(8,128)(2,1)} %multiply_convert_fusion.4.queries, bf16[768,128]{1,0:T(8,128)(2,1)} %fusion.97.extra, bf16[3072,768]{1,0:T(8,128)(2,1)} %convolution_convert_fusion.4.keys, bf16[768,3072]{1,0:T(8,128)(2,1)} %convolution_convert_fusion.3.values_t, ...), custom_call_target="tpu_custom_call" | custom-call | flops 28991029248 | bytes 37748736 | tf_op jit(solution)/shard_map/attention_forward/pallas_call | solution.py:158
  217.9 3.0 multiply_reduce_fusion.3
  221.0 9.6 %fusion.98 = f32[768,3072]{1,0:T(8,128)} fusion(bf16[768,3072]{1,0:T(8,128)(2,1)} %bitcast.193, f32[768,768]{1,0:T(8,128)S(1)} %get-tuple-element.113, f32[768]{0:T(1024)S(1)} %get-tuple-element.66, f32[768]{0:T(1024)S(1)} %fusion.86), kind=kOutput, calls=%fused_computation.210 | convolution fusion | flops 3625648128 | bytes 16521216 | tf_op jit(solution)/shard_map/dot_general | solution.py:34
  230.6 12.5 %fusion.3 = bf16[768,3072]{1,0:T(8,128)(2,1)S(1)} fusion(f32[768,3072]{1,0:T(8,128)} %fusion.98, bf16[3072,768]{1,0:T(8,128)(2,1)S(1)} %bitcast.189, bf16[1,768,768]{2,1,0:T(8,128)(2,1)S(1)} %copy-done.10), kind=kOutput, calls=%fused_computation.9 | convolution fusion | flops 3680501760 | bytes 20054016 | tf_op jit(solution)/shard_map/dot_general | solution.py:34
  243.2 4.1 multiply_reduce_fusion.1
  248.0 2.2 convolution_convert_fusion.8.context_grad
  250.1 2.9 convert_multiply_fusion.4
  256.0 9.6 %select_convert_fusion = (bf16[12,768,128]{2,1,0:T(8,128)(2,1)}, bf16[12,768,128]{2,1,0:T(8,128)(2,1)}) fusion(bf16[12,768]{1,0:T(8,128)(2,1)S(1)} %get-tuple-element.97, bf16[12,768]{1,0:T(8,128)(2,1)S(1)} %get-tuple-element.96, bf16[12,768]{1,0:T(8,128)(2,1)S(1)} %get-tuple-element.95, pred[128]{0:T(512)(128)(4,1)S(1)} %get-tuple-element.124, ...), kind=kLoop, calls=%fused_computation.31 | loop fusion | flops 7077888 | bytes 5026176 | tf_op jit(solution)/shard_map/convert_element_type | solution.py:94
  265.6 75.7 %attention_backward.1 = (f32[768,768]{1,0:T(8,128)}, bf16[768,3072]{1,0:T(8,128)(2,1)}, bf16[768,3072]{1,0:T(8,128)(2,1)}, f32[12,6,3072]{2,1,0:T(8,128)}) custom-call(bf16[768,768]{1,0:T(8,128)(2,1)} %multiply_convert_fusion.4.queries, bf16[12,768,128]{2,1,0:T(8,128)(2,1)} %get-tuple-element.107.query_rows, ...), custom_call_target="tpu_custom_call" | custom-call | flops 56623104000 | bytes 75497472 | tf_op jit(solution)/shard_map/attention_backward/pallas_call | solution.py:245
  341.3 6.0 fusion.51
  347.4 6.1 add_convert_fusion
  353.5 6.7 %copy.61 = bf16[768,3072]{1,0:T(8,128)(2,1)} copy(bf16[768,3072]{0,1:T(8,128)(2,1)} %bitcast.163) | data formatting | bytes 9437184 | tf_op jit(solution)/shard_map/dot_general | solution.py:34
  360.3 5.4 fusion.46
  365.6 2.1 convolution_convert_fusion.5
  367.8 9.2 %convolution_convert_fusion.2 = bf16[768,3072]{1,0:T(8,128)(2,1)} fusion(bf16[768,3072]{1,0:T(8,128)(2,1)} %copy-done.56, f32[768,768]{1,0:T(8,128)S(1)} %copy-done.9, f32[768]{0:T(1024)S(1)} %get-tuple-element.66, f32[768]{0:T(1024)S(1)} %fusion.86), kind=kOutput, calls=%fused_computation.24 | convolution fusion | flops 3628007424 | bytes 11802624 | tf_op jit(solution)/shard_map/dot_general | solution.py:34
  377.0 4.9 fusion.28
  382.0 4.9 fusion.31
  386.9 7.1 %convolution_convert_fusion.1 = bf16[3072,768]{1,0:T(8,128)(2,1)} fusion(bf16[1,768,768]{2,1,0:T(8,128)(2,1)S(1)} %copy-done.11, f32[768,3072]{1,0:T(8,128)S(1)} %bitcast.206), kind=kOutput, calls=%fused_computation.23 | convolution fusion | flops 3647471616 | bytes 15335424 | tf_op jit(solution)/shard_map/dot_general | solution.py:34
  394.0 6.9 %fusion.34 = bf16[1,768,768]{2,1,0:T(8,128)(2,1)} fusion(f32[768,768]{1,0:T(8,128)S(1)} %copy-done.9, bf16[3072,768]{1,0:T(8,128)(2,1)S(1)} %bitcast.192, f32[768,3072]{1,0:T(8,128)S(1)} %bitcast.206), kind=kOutput, calls=%fused_computation.73 | convolution fusion | flops 3646291968 | bytes 17694720 | tf_op jit(solution)/shard_map/dot_general | solution.py:34
  401.0 45.6 %reduce-scatter.2.cloned.1.call-done = bf16[768,768]{1,0:T(8,128)(2,1)} async-done(((bf16[3072,768]{1,0:T(8,128)(2,1)}), bf16[768,768]{1,0:T(8,128)(2,1)}) %reduce-scatter.2.cloned.1.call-update) | async-done | bytes 1179664 | tf_op jit(solution)/shard_map/reduce_scatter | solution.py:762
  446.6 3.9 fusion.22
  450.5 2.3 fusion.99
  458.6 94.3 %scatter_terms.1 = (f32[24,2304]{1,0:T(8,128)}, f32[24,768]{1,0:T(8,128)}, f32[24,3072]{1,0:T(8,128)}, f32[96,768]{1,0:T(8,128)}) custom-call(bf16[4,2,2,48,2304]{4,3,2,1,0:T(8,128)(2,1)} %pad_maximum_fusion.refs_0_, bf16[4,2,2,48,768]{4,3,2,1,0:T(8,128)(2,1)} %bitcast.168, bf16[4,2,2,48,3072]{4,3,2,1,0:T(8,128)(2,1)} %bitcast.166, ...), custom_call_target="tpu_custom_call" | custom-call | tf_op jit(solution)/shard_map/scatter_terms/pallas_call | solution.py:620
  562.6 2.7 pad_maximum_fusion.3
  565.3 41.3 %all-reduce = (f32[2,768]{1,0:T(2,128)S(1)}, f32[32,12]{0,1:T(8,128)S(1)}, f32[4]{0:T(128)S(1)}, f32[2304]{0:T(1024)S(1)}, f32[768]{0:T(1024)S(1)}, /*index=5*/f32[3072]{0:T(1024)S(1)}, f32[768]{0:T(1024)S(1)}) all-reduce(f32[2,768]{1,0:T(2,128)S(1)} %pad_maximum_fusion.2, ...), channel_id=1, replica_groups=mesh['seq'=4,'dp'=8] {'seq','dp'}, use_global_device_ids=true, to_apply=%region_11.12 | all-reduce | flops 8836 | bytes 70688 | tf_op jit(solution)/shard_map/psum | solution.py:790
  (230 shorter events, 33.2 us)
Async XLA Ops:
  7.2 133.3 %copy-start.2 = (bf16[1,768,768]{2,1,0:T(8,128)(2,1)S(1)}, bf16[1,768,768]{2,1,0:T(8,128)(2,1)}, u32[]{:S(2)}) copy-start(bf16[1,768,768]{2,1,0:T(8,128)(2,1)} %param.20) | copy-start | bytes 3538948
  7.2 439.4 %reduce-scatter.2.cloned.1.call-start = ((), (), s32[]{:S(2)}) async-start(), calls=%async_computation.1 | async-start | bytes 5898240 | tf_op jit(solution)/shard_map/reduce_scatter | solution.py:762
  9.7 134.2 %copy-start.35 = (f32[768]{0:T(1024)}, f32[768]{0:T(1024)S(1)}, u32[]{:S(2)}) copy-start(f32[768]{0:T(1024)S(1)} %fusion.85) | copy-start | bytes 9220
  10.5 138.2 %copy-start.26 = (f32[768]{0:T(1024)}, f32[768]{0:T(1024)S(1)}, u32[]{:S(2)}) copy-start(f32[768]{0:T(1024)S(1)} %get-tuple-element.67) | copy-start | bytes 9220
  265.6 75.7 %copy-start.53 = (bf16[4,2,2,48,2304]{4,3,2,1,0:T(8,128)(2,1)S(1)}, bf16[4,2,2,48,2304]{4,3,2,1,0:T(8,128)(2,1)}, u32[]{:S(2)}) copy-start(bf16[4,2,2,48,2304]{4,3,2,1,0:T(8,128)(2,1)} %get-tuple-element.39) | copy-start | bytes 10616836
  394.0 52.6 %copy-start.3 = (bf16[1,768,768]{2,1,0:T(8,128)(2,1)S(1)}, bf16[1,768,768]{2,1,0:T(8,128)(2,1)}, u32[]{:S(2)}) copy-start(bf16[1,768,768]{2,1,0:T(8,128)(2,1)} %param.20) | copy-start | bytes 3538948
  394.0 52.6 %copy-start.27 = (f32[768]{0:T(1024)S(1)}, f32[768]{0:T(1024)}, u32[]{:S(2)}) copy-start(f32[768]{0:T(1024)} %copy-done.26) | copy-start | bytes 9220
  394.0 52.6 %copy-start.36 = (f32[768]{0:T(1024)S(1)}, f32[768]{0:T(1024)}, u32[]{:S(2)}) copy-start(f32[768]{0:T(1024)} %copy-done.35) | copy-start | bytes 9220
  458.4 101.7 %copy-start.48 = (f32[24]{0:T(128)S(1)}, f32[24]{0:T(128)}, u32[]{:S(2)}) copy-start(f32[24]{0:T(128)} %param.32) | copy-start | bytes 292
  458.4 102.4 %copy-start.49 = (f32[24]{0:T(128)S(1)}, f32[24]{0:T(128)}, u32[]{:S(2)}) copy-start(f32[24]{0:T(128)} %param.30) | copy-start | bytes 292
  458.4 103.0 %copy-start.50 = (f32[96]{0:T(128)S(1)}, f32[96]{0:T(128)}, u32[]{:S(2)}) copy-start(f32[96]{0:T(128)} %param.36) | copy-start | bytes 1156
  458.4 103.6 %copy-start.51 = (f32[24]{0:T(128)S(1)}, f32[24]{0:T(128)}, u32[]{:S(2)}) copy-start(f32[24]{0:T(128)} %param.34) | copy-start | bytes 292
  458.4 106.8 %copy-start.40 = (f32[12,32]{1,0:T(8,128)S(1)}, f32[12,32]{1,0:T(8,128)}, u32[]{:S(2)}) copy-start(f32[12,32]{1,0:T(8,128)} %fusion.46) | copy-start | bytes 4612
  458.5 151.3 %copy-start.42 = (f32[768]{0:T(1024)S(1)}, f32[768]{0:T(1024)}, u32[]{:S(2)}) copy-start(f32[768]{0:T(1024)} %param.33) | copy-start | bytes 9220
  458.5 151.4 %copy-start.43 = (f32[768]{0:T(1024)S(1)}, f32[768]{0:T(1024)}, u32[]{:S(2)}) copy-start(f32[768]{0:T(1024)} %param.37) | copy-start | bytes 9220
  458.5 151.4 %copy-start.37 = (f32[2304]{0:T(1024)S(1)}, f32[2304]{0:T(1024)}, u32[]{:S(2)}) copy-start(f32[2304]{0:T(1024)} %param.31) | copy-start | bytes 27652
  458.5 151.4 %copy-start.38 = (f32[3072]{0:T(1024)S(1)}, f32[3072]{0:T(1024)}, u32[]{:S(2)}) copy-start(f32[3072]{0:T(1024)} %param.35) | copy-start | bytes 36868
  458.5 151.4 %copy-start.32 = (f32[2,768]{1,0:T(2,128)S(1)}, f32[2,768]{1,0:T(2,128)}, u32[]{:S(2)}) copy-start(f32[2,768]{1,0:T(2,128)} %param.24) | copy-start | bytes 18436
  458.5 151.4 %copy-start.41 = (f32[2,768]{1,0:T(2,128)S(1)}, f32[2,768]{1,0:T(2,128)}, u32[]{:S(2)}) copy-start(f32[2,768]{1,0:T(2,128)} %param.38) | copy-start | bytes 18436
  458.5 152.1 %copy-start.31 = (f32[32,12]{0,1:T(8,128)S(1)}, f32[32,12]{0,1:T(8,128)}, u32[]{:S(2)}) copy-start(f32[32,12]{0,1:T(8,128)} %param.25) | copy-start | bytes 4612
  458.5 152.0 %copy-start.39 = (f32[32,12]{0,1:T(8,128)S(1)}, f32[32,12]{0,1:T(8,128)}, u32[]{:S(2)}) copy-start(f32[32,12]{0,1:T(8,128)} %param.39) | copy-start | bytes 4612
  458.6 152.6 %copy-start.22 = (f32[24,768]{1,0:T(8,128)S(1)}, f32[24,768]{1,0:T(8,128)}, u32[]{:S(2)}) copy-start(f32[24,768]{1,0:T(8,128)} %refs_1_.1) | copy-start | bytes 221188
  552.9 59.9 %copy-start.16 = (f32[96,768]{1,0:T(8,128)S(1)}, f32[96,768]{1,0:T(8,128)}, u32[]{:S(2)}) copy-start(f32[96,768]{1,0:T(8,128)} %get-tuple-element.53) | copy-start | bytes 884740
  552.9 59.9 %copy-start.17 = (f32[96,768]{1,0:T(8,128)S(1)}, f32[96,768]{1,0:T(8,128)}, u32[]{:S(2)}) copy-start(f32[96,768]{1,0:T(8,128)} %refs_3_.1) | copy-start | bytes 884740
  552.9 60.7 %copy-start.19 = (f32[24,2304]{1,0:T(8,128)S(1)}, f32[24,2304]{1,0:T(8,128)}, u32[]{:S(2)}) copy-start(f32[24,2304]{1,0:T(8,128)} %get-tuple-element.50) | copy-start | bytes 663556
  553.0 60.7 %copy-start.20 = (f32[24,2304]{1,0:T(8,128)S(1)}, f32[24,2304]{1,0:T(8,128)}, u32[]{:S(2)}) copy-start(f32[24,2304]{1,0:T(8,128)} %refs_0_.1) | copy-start | bytes 663556
  553.0 61.5 %copy-start.15 = (f32[24,3072]{1,0:T(8,128)S(1)}, f32[24,3072]{1,0:T(8,128)}, u32[]{:S(2)}) copy-start(f32[24,3072]{1,0:T(8,128)} %get-tuple-element.52) | copy-start | bytes 884740
  553.0 61.5 %copy-start.18 = (f32[24,3072]{1,0:T(8,128)S(1)}, f32[24,3072]{1,0:T(8,128)}, u32[]{:S(2)}) copy-start(f32[24,3072]{1,0:T(8,128)} %refs_2_.1) | copy-start | bytes 884740
  560.8 54.5 %copy-start.44 = (f32[24]{0:T(128)}, f32[24]{0:T(128)S(1)}, u32[]{:S(2)}) copy-start(f32[24]{0:T(128)S(1)} %get-tuple-element.85) | copy-start | bytes 292
  561.4 53.9 %copy-start.47 = (f32[24]{0:T(128)}, f32[24]{0:T(128)S(1)}, u32[]{:S(2)}) copy-start(f32[24]{0:T(128)S(1)} %get-tuple-element.82) | copy-start | bytes 292
  562.0 53.3 %copy-start.45 = (f32[96]{0:T(128)}, f32[96]{0:T(128)S(1)}, u32[]{:S(2)}) copy-start(f32[96]{0:T(128)S(1)} %get-tuple-element.91) | copy-start | bytes 1156
  562.6 52.7 %copy-start.46 = (f32[24]{0:T(128)}, f32[24]{0:T(128)S(1)}, u32[]{:S(2)}) copy-start(f32[24]{0:T(128)S(1)} %get-tuple-element.88) | copy-start | bytes 292
  (42 other events, 349.6 us)
Sparse Core Ops, SparseCore 0:
  353.6 92.9 reduce-scatter.1

commit v3 on v1

--- a/solution.py
+++ b/solution.py
@@ -1,3 +1,4 @@
+import functools
 import math
 
 import jax
@@ -182,6 +183,723 @@
     )(queries, extra, keys, values_t, keys_extra)
 
 
+MESH = pl.DeviceIdType.MESH
+
+
+class Place:
+    def __init__(self):
+        self.seq, self.dp = lax.axis_index("seq"), lax.axis_index("dp")
+        self.core, self.x, self.y = self.dp % 2, self.dp // 2 % 2, self.dp // 4
+        self.by_core = (self.seq, self.dp + 1 - 2 * self.core)
+        self.by_x = (self.seq, self.dp + 2 - 4 * self.x)
+        self.by_y = (self.seq, self.dp + 4 - 8 * self.y)
+        self.others = [((self.seq + step) % 4, self.dp) for step in (1, 2, 3)]
+
+    def greet(self):
+        barrier = pltpu.get_barrier_semaphore()
+        partners = [self.by_core, self.by_x, self.by_y] + self.others
+        for partner in partners:
+            pl.semaphore_signal(barrier, inc=1, device_id=partner, device_id_type=MESH)
+        pl.semaphore_wait(barrier, len(partners))
+
+
+def send(source, target, sems, index, partner):
+    return pltpu.make_async_remote_copy(
+        src_ref=source,
+        dst_ref=target,
+        send_sem=sems.at[0, index],
+        recv_sem=sems.at[1, index],
+        device_id=partner,
+        device_id_type=MESH,
+    )
+
+
+def half_of(width, which):
+    return pl.ds(pl.multiple_of(which * (width // 2), 128), width // 2)
+
+
+class Gather:
+    steps = 6
+
+    def __init__(self, at, shard, pair, low, whole, sems, local_sems, x_first):
+        self.at, self.shard, self.pair, self.low, self.whole = at, shard, pair, low, whole
+        rows, width = shard.shape
+        mine, other = half_of(width, at.core), half_of(width, 1 - at.core)
+        own_rows = pl.ds(pl.multiple_of(rows * at.core, 8), rows)
+        place = whole.at[at.seq, at.y, at.x, :, mine]
+        along_x, along_y = (whole.at[:, at.y, at.x, :, mine], whole.at[:, at.y, :, :, mine])
+        if not x_first:
+            along_x, along_y = (whole.at[:, :, at.x, :, mine], along_x)
+        self.local = [
+            pltpu.make_async_copy(shard.at[:, mine], pair.at[own_rows], local_sems.at[0]),
+            pltpu.make_async_copy(low, place, local_sems.at[1]),
+        ]
+        self.first = send(shard.at[:, other], pair.at[own_rows], sems, 0, at.by_core)
+        self.over_z = [send(low, place, sems, 1 + k, at.others[k]) for k in range(3)]
+        self.over_x = send(along_x, along_x, sems, 4, at.by_x)
+        self.over_y = send(along_y, along_y, sems, 5, at.by_y)
+        self.order = [self.over_x, self.over_y] if x_first else [self.over_y, self.over_x]
+        self.last = send(whole.at[:, :, :, :, mine], whole.at[:, :, :, :, mine], sems, 6, at.by_core)
+
+    def step(self, number):
+        if number == 0:
+            self.local[0].start()
+            self.first.start()
+        elif number == 1:
+            self.local[0].wait()
+            self.first.wait()
+            self.low[...] = self.pair[...].astype(low_type)
+            self.local[1].start()
+            for copy in self.over_z:
+                copy.start()
+        elif number == 2:
+            self.local[1].wait()
+            for copy in self.over_z:
+                copy.wait()
+            self.order[0].start()
+        elif number == 3:
+            self.order[0].wait()
+            self.order[1].start()
+        elif number == 4:
+            self.order[1].wait()
+            self.last.start()
+        else:
+            self.last.wait()
+
+
+class Scatter:
+    steps = 6
+
+    def __init__(self, at, plan, term, share, scratch, sems):
+        start, width, share_start, self.x_first = plan
+        self.at, self.held, self.arrived, self.total = at, scratch[0], scratch[1:5], scratch[5]
+        held, arrived, total, x_first = self.held, self.arrived, self.total, self.x_first
+        sems, local_sems = sems
+        rows = term.shape[3] // 2
+        columns = lambda first, which: pl.ds(
+            pl.multiple_of(first + which * (width // 2), 128), width // 2
+        )
+        mine, other = columns(start, at.core), columns(start, 1 - at.core)
+        share_mine = columns(share_start, at.core)
+        of_core = lambda which: pl.ds(pl.multiple_of(rows * which, 8), rows)
+        self.local = [
+            pltpu.make_async_copy(term.at[:, :, :, :, mine], held, local_sems.at[0]),
+            pltpu.make_async_copy(
+                total.at[of_core(at.core)], share.at[:, share_mine], local_sems.at[1]
+            ),
+        ]
+        self.first = send(term.at[:, :, :, :, other], arrived[0], sems, 0, at.by_core)
+        if x_first:
+            self.second = send(held.at[:, :, 1 - at.x], arrived[1], sems, 1, at.by_x)
+            self.third = send(held.at[:, 1 - at.y, at.x], arrived[2], sems, 2, at.by_y)
+        else:
+            self.second = send(held.at[:, 1 - at.y], arrived[1], sems, 1, at.by_y)
+            self.third = send(held.at[:, at.y, 1 - at.x], arrived[2], sems, 2, at.by_x)
+        self.over_z = [
+            send(held.at[at.others[k][0], at.y, at.x], arrived[3].at[k], sems, 3 + k, at.others[k])
+            for k in range(3)
+        ]
+        self.last = send(
+            total.at[of_core(1 - at.core)], share.at[:, share_mine], sems, 6, at.by_core
+        )
+
+    def add(self, place, values):
+        self.held[place] = (self.held[place].astype(f32) + values.astype(f32)).astype(low_type)
+
+    def step(self, number):
+        at = self.at
+        if number == 0:
+            self.local[0].start()
+            self.first.start()
+        elif number == 1:
+            self.local[0].wait()
+            self.first.wait()
+
+            @pl.loop(0, 4)
+            def _(row):
+                for across in range(4):
+                    place = (row, across // 2, across % 2)
+                    self.add(place, self.arrived[0][place])
+
+            self.second.start()
+        elif number == 2:
+            self.second.wait()
+
+            @pl.loop(0, 4)
+            def _(row):
+                for across in range(2):
+                    place = (row, across, at.x) if self.x_first else (row, at.y, across)
+                    self.add(place, self.arrived[1][row, across])
+
+            self.third.start()
+        elif number == 3:
+            self.third.wait()
+
+            @pl.loop(0, 4)
+            def _(row):
+                self.add((row, at.y, at.x), self.arrived[2][row])
+
+            for copy in self.over_z:
+                copy.start()
+        elif number == 4:
+            for copy in self.over_z:
+                copy.wait()
+            total = self.held[at.seq, at.y, at.x].astype(f32)
+            for k in range(3):
+                total = total + self.arrived[3][k].astype(f32)
+            self.total[...] = total
+            self.local[1].start()
+            self.last.start()
+        else:
+            self.local[1].wait()
+            self.last.wait()
+
+
+class Ring:
+    def __init__(self, at, own, blocks, sems, local_sem):
+        self.at = at
+        seq = at.seq
+        self.local = pltpu.make_async_copy(own, blocks.at[seq], local_sem)
+        right, left = ((seq + 1) % 4, at.dp), ((seq + 3) % 4, at.dp)
+        self.hops = []
+        for hop in range(3):
+            back, ahead = (seq + 4 - hop) % 4, (seq + hop) % 4
+            block_back = own if hop == 0 else blocks.at[back]
+            block_ahead = own if hop == 0 else blocks.at[ahead]
+            self.hops.append(
+                [
+                    (
+                        (seq >= hop) & (seq < 3),
+                        send(block_back, blocks.at[back], sems, hop, right),
+                        seq >= hop + 1,
+                    ),
+                    (
+                        (seq + hop <= 3) & (seq > 0),
+                        send(block_ahead, blocks.at[ahead], sems, 3 + hop, left),
+                        seq + hop + 1 <= 3,
+                    ),
+                ]
+            )
+
+    def start(self, hop):
+        if hop == 0:
+            self.local.start()
+        for sends, copy, _ in self.hops[hop]:
+            pl.when(sends)(copy.start)
+
+    def arrive(self, hop):
+        for _, copy, receives in self.hops[hop]:
+            pl.when(receives)(copy.wait_recv)
+
+    def finish(self):
+        for hop in self.hops:
+            for sends, copy, _ in hop:
+                pl.when(sends)(copy.wait_send)
+
+
+X_FIRST = (True, False, False, True)
+
+
+def remote_scratch(shapes):
+    return [pltpu.SemaphoreType.DMA((2, 7)), pltpu.SemaphoreType.DMA((2,))] * len(shapes)
+
+
+def opening_kernel(*refs):
+    shards, own = refs[:4], refs[4]
+    gains, bucket_rows, bias_table, lengths = refs[5:9]
+    wholes, outs = refs[9:13], refs[13:21]
+    normed_out, keys_out, values_out, keys_extra_out, queries, queries_t, context_t, log_total = outs
+    extra = refs[21]
+    scratch = refs[22:]
+    pairs, lows, sems = scratch[:4], scratch[4:8], scratch[8:16]
+    ring_sems, ring_local, out_sems, blocks, project, normed, keys, values_t = scratch[16:24]
+    keys_extra, picks, sums, tops = scratch[24:]
+    at = Place()
+    at.greet()
+    gathers = [
+        Gather(
+            at,
+            shards[k],
+            pairs[k],
+            lows[k],
+            project if k == 0 else wholes[k],
+            sems[2 * k],
+            sems[2 * k + 1],
+            X_FIRST[k],
+        )
+        for k in range(4)
+    ]
+    first, rest = gathers[0], gathers[1:]
+    ring = Ring(at, own, blocks, ring_sems, ring_local.at[0])
+
+    def rest_step(number):
+        for gather in rest:
+            gather.step(number)
+
+    for gather in gathers:
+        gather.step(0)
+    first.step(1)
+    rest_step(1)
+
+    count, buckets = own.shape[0], bias_table.shape[0]
+    row_length = keys_extra.shape[0]
+    query_blocks = count // BLK
+    doc_start, one_start = extra_columns(query_blocks)
+    picked = query_blocks * buckets
+    ends = []
+    for doc in range(DOCS):
+        ends.append(lengths[0, doc] + (ends[-1] if ends else 0))
+
+    def documents_at(position):
+        return sum((position >= end).astype(jnp.int32) for end in ends)
+
+    bucket_at = lax.broadcasted_iota(jnp.int32, (buckets, row_length), 0)
+    for block in range(query_blocks):
+        picks[buckets * block : buckets * block + buckets, :] = (
+            (bucket_rows[block : block + 1, :] == bucket_at).astype(f32).astype(low_type)
+        )
+    last = picks.shape[0] - picked
+    row = lax.broadcasted_iota(jnp.int32, (last, row_length), 0)
+    key_doc = documents_at(lax.broadcasted_iota(jnp.int32, (last, row_length), 1))
+    picks[picked:, :] = (
+        jnp.where(row < DOCS, (key_doc != row).astype(f32), (row == DOCS).astype(f32))
+    ).astype(low_type)
+
+    table = jnp.concatenate([bias_table[...]] * query_blocks, axis=0)
+    table_lane = lax.broadcasted_iota(jnp.int32, table.shape, 1)
+    lane = lax.broadcasted_iota(jnp.int32, (picked, 128), 1)
+    lane_block = lax.broadcasted_iota(jnp.int32, (picked, 128), 0) // buckets
+    lane_last = lax.broadcasted_iota(jnp.int32, (last, 128), 1)
+    row_last = lax.broadcasted_iota(jnp.int32, (last, 128), 0)
+    below = jnp.where(
+        (row_last < DOCS) & (lane_last - doc_start == row_last),
+        masked_score,
+        jnp.where(
+            (row_last == DOCS) & (lane_last >= one_start) & (lane_last < one_start + TERMS), 1.0, 0.0
+        ),
+    ).astype(low_type)
+
+    @pl.loop(0, PAIRS)
+    def _(pair):
+        sides = []
+        for head in range(2):
+            rest_of = jnp.sum(
+                jnp.where(table_lane == 2 * pair + head, table, 0.0), axis=1, keepdims=True
+            )
+            side = jnp.zeros((picked, 128), f32)
+            for term in range(TERMS):
+                part = rest_of.astype(low_type).astype(f32)
+                rest_of = rest_of - part
+                side = jnp.where(lane == term * query_blocks + lane_block, part, side)
+            sides.append(jnp.concatenate([side.astype(low_type), below], axis=0))
+        keys_extra[:, pl.ds(pl.multiple_of(256 * pair, 256), 256)] = dot(
+            picks[...], jnp.concatenate(sides, axis=1), 0, 0
+        ).astype(low_type)
+
+    extra_lane = lax.broadcasted_iota(jnp.int32, (count, 128), 1)
+    extra_row = lax.broadcasted_iota(jnp.int32, (count, 128), 0)
+    query_doc = documents_at(extra_row + at.seq * count)
+    extra[...] = (
+        (
+            ((extra_lane < doc_start) & (extra_lane % query_blocks == extra_row // BLK))
+            | ((extra_lane < one_start) & (extra_lane - doc_start == query_doc))
+        )
+        .astype(f32)
+        .astype(low_type)
+    )
+    sums[...] = jnp.zeros_like(sums)
+    tops[...] = jnp.full_like(tops, masked_score)
+
+    first.step(2)
+    ring.start(0)
+    first.step(3)
+    ring.local.wait()
+    first.step(4)
+    first.step(5)
+
+    copies = [
+        pltpu.make_async_copy(keys_extra, keys_extra_out, out_sems.at[0]),
+        pltpu.make_async_copy(project, wholes[0], out_sems.at[1]),
+    ]
+    for copy in copies:
+        copy.start()
+    weights = [project[:, :, :, :, D * part : D * part + D].reshape(D, D) for part in range(3)]
+    pair_lane = lax.broadcasted_iota(jnp.int32, (count, PAIR), 1)
+
+    def attend_pair(block, pair):
+        lanes = pl.ds(pl.multiple_of(pair * PAIR, PAIR), PAIR)
+        key_rows = pl.ds(pl.multiple_of(block * count, count), count)
+        query_pair, key_pair = queries[:, lanes], keys[block, :, lanes]
+        for head in range(2):
+            which = 2 * pair + head
+            mine = (pair_lane < HEAD) if head == 0 else (pair_lane >= HEAD)
+            query_side = jnp.concatenate(
+                [jnp.where(mine, query_pair, jnp.zeros_like(query_pair)), extra[...]], axis=1
+            )
+            more = keys_extra[key_rows, pl.ds(pl.multiple_of(128 * which, 128), 128)]
+            scores = dot(jnp.concatenate([key_pair, more], axis=1), query_side, 1, 1)
+            top_before = tops[which, 0:1]
+            top = jnp.maximum(top_before, jnp.max(scores, axis=0, keepdims=True))
+            unscaled = jnp.exp(scores - top).astype(low_type)
+            value_side = jnp.concatenate(
+                [
+                    values_t[block, pl.ds(pl.multiple_of(HEAD * which, HEAD), HEAD), :],
+                    jnp.ones((16, count), low_type),
+                ],
+                axis=0,
+            )
+            sums[which] = sums[which] * jnp.exp(top_before - top) + dot(value_side, unscaled, 1, 0)
+            tops[which] = jnp.broadcast_to(top, (8, count))
+
+    side = at.seq // 2
+    order = [at.seq, 1 - at.seq + 4 * side, 2 - side, 3 - 3 * side]
+    events = {
+        (0, 1): [lambda: (ring.arrive(0), ring.start(1))],
+        (0, 3): [lambda: rest_step(2)],
+        (1, 1): [lambda: rest_step(3)],
+        (1, 5): [lambda: (ring.arrive(1), ring.start(2))],
+        (2, 5): [lambda: (ring.arrive(2), rest_step(4))],
+    }
+    for slot, block in enumerate(order):
+        values = blocks[block].astype(f32)
+        normed_low = (
+            values
+            * lax.rsqrt(jnp.mean(values * values, axis=1, keepdims=True) + norm_epsilon)
+            * gains[0:1, :]
+        ).astype(low_type)
+        normed[block] = normed_low
+        keys[block] = dot(normed_low, weights[1], 1, 0).astype(low_type)
+        values_t[block] = dot(weights[2], normed_low, 0, 1).astype(low_type)
+        for place, (source, target) in enumerate(
+            ((normed, normed_out), (keys, keys_out), (values_t, values_out))
+        ):
+            copy = pltpu.make_async_copy(
+                source.at[block], target.at[block], out_sems.at[2 + 3 * slot + place]
+            )
+            copy.start()
+            copies.append(copy)
+        if slot == 0:
+            scaled = lambda values: (values.astype(low_type).astype(f32) * score_scale).astype(low_type)
+            queries[...] = scaled(dot(normed_low, weights[0], 1, 0))
+            queries_t[...] = scaled(dot(weights[0], normed_low, 0, 1))
+
+        @pl.loop(0, PAIRS)
+        def _(pair, slot=slot, block=block):
+            for (when, which), actions in events.items():
+                if when == slot:
+
+                    @pl.when(pair == which)
+                    def _(actions=actions):
+                        for action in actions:
+                            action()
+
+            attend_pair(block, pair)
+
+    for head in range(HEADS):
+        total = sums[head, HEAD : HEAD + 1]
+        context_t[HEAD * head : HEAD * head + HEAD, :] = sums[head, :HEAD] / total
+        log_total[head : head + 1, :] = tops[head, 0:1] + jnp.log(total)
+    rest_step(5)
+    ring.finish()
+    for copy in copies:
+        copy.wait()
+
+
+def open_layer(shards, own, gains, bucket_rows, bias_table, lengths):
+    low_shape = lambda shard: (2 * shard.shape[0], shard.shape[1] // 2)
+    anywhere = pl.BlockSpec(memory_space=pl.ANY)
+    in_place = pl.BlockSpec(memory_space=pltpu.VMEM)
+    count, blocks = own.shape[0], bucket_rows.shape[0]
+    row_length = 4 * count
+    picked = blocks * bias_table.shape[0] + 16
+    low = lambda *shape: jax.ShapeDtypeStruct(shape, low_type)
+    whole_shapes = [(4, 2, 2, 2 * shard.shape[0], shard.shape[1]) for shard in shards]
+    return pl.pallas_call(
+        opening_kernel,
+        out_shape=[low(*shape) for shape in whole_shapes]
+        + [low(4, count, D)] * 2
+        + [low(4, D, count), low(row_length, HEADS * 128), low(count, D), low(D, count)]
+        + [jax.ShapeDtypeStruct((D, count), f32), jax.ShapeDtypeStruct((16, count), f32)]
+        + [low(count, 128)],
+        in_specs=[anywhere] * 5 + [in_place] * 3 + [pl.BlockSpec(memory_space=pltpu.SMEM)],
+        out_specs=[anywhere] * 8 + [in_place] * 5,
+        scratch_shapes=[pltpu.VMEM(low_shape(shard), f32) for shard in shards]
+        + [pltpu.VMEM(low_shape(shard), low_type) for shard in shards]
+        + remote_scratch(shards)
+        + [
+            pltpu.SemaphoreType.DMA((2, 6)),
+            pltpu.SemaphoreType.DMA((1,)),
+            pltpu.SemaphoreType.DMA((14,)),
+            pltpu.VMEM((4, count, D), low_type),
+            pltpu.VMEM(whole_shapes[0], low_type),
+            pltpu.VMEM((4, count, D), low_type),
+            pltpu.VMEM((4, count, D), low_type),
+            pltpu.VMEM((4, D, count), low_type),
+            pltpu.VMEM((row_length, HEADS * 128), low_type),
+            pltpu.VMEM((picked, row_length), low_type),
+            pltpu.VMEM((HEADS, HEAD + 16, count), f32),
+            pltpu.VMEM((HEADS, 8, count), f32),
+        ],
+        compiler_params=pltpu.CompilerParams(
+            collective_id=0, has_side_effects=True, vmem_limit_bytes=vmem_bytes
+        ),
+        name="open_layer",
+    )(*shards, own, gains, bucket_rows, bias_table, lengths)
+
+
+def scatter_scratch(terms, plans):
+    buffers, sems = [], []
+    for term, (_, width, _, _) in zip(terms, plans):
+        rows, half = term.shape[3], width // 2
+        buffers += [
+            pltpu.VMEM((4, 2, 2, rows, half), low_type),
+            pltpu.VMEM((4, 2, 2, rows, half), low_type),
+            pltpu.VMEM((4, 2, rows, half), low_type),
+            pltpu.VMEM((4, rows, half), low_type),
+            pltpu.VMEM((3, rows, half), low_type),
+            pltpu.VMEM((rows, half), f32),
+        ]
+        sems += [pltpu.SemaphoreType.DMA((2, 7)), pltpu.SemaphoreType.DMA((2,))]
+    return buffers + sems
+
+
+def make_scatters(at, plans, terms, shares, scratch):
+    buffers, sems = scratch[: 6 * len(plans)], scratch[6 * len(plans) :]
+    return [
+        Scatter(
+            at,
+            plans[k],
+            terms[k],
+            shares[k],
+            buffers[6 * k : 6 * k + 6],
+            sems[2 * k : 2 * k + 2],
+        )
+        for k in range(len(plans))
+    ]
+
+
+def by_chip(term):
+    return term.reshape(4, 2, 2, term.shape[0] // 16, term.shape[1])
+
+
+class AllSum:
+    def __init__(self, at, own, arrived, summed, rows, sems):
+        self.at, self.own, self.arrived, self.summed, self.rows = at, own, arrived, summed, rows
+        place = rows.at[at.seq]
+        self.by_core = send(own, arrived.at[0], sems, 0, at.by_core)
+        self.by_x = send(summed.at[0], arrived.at[1], sems, 1, at.by_x)
+        self.by_y = send(summed.at[1], arrived.at[2], sems, 2, at.by_y)
+        self.over_z = [send(place, place, sems, 3 + k, at.others[k]) for k in range(3)]
+
+    def step(self, number):
+        if number == 0:
+            self.by_core.start()
+        elif number == 1:
+            self.by_core.wait()
+            self.summed[0] = self.own[...] + self.arrived[0]
+            self.by_x.start()
+        elif number == 2:
+            self.by_x.wait()
+            self.summed[1] = self.summed[0] + self.arrived[1]
+            self.by_y.start()
+        elif number == 3:
+            self.by_y.wait()
+            self.rows[self.at.seq] = self.summed[1] + self.arrived[2]
+            for copy in self.over_z:
+                copy.start()
+        else:
+            for copy in self.over_z:
+                copy.wait()
+
+    def total(self):
+        return (self.rows[0] + self.rows[1]) + (self.rows[2] + self.rows[3])
+
+
+def sum_scratch(width):
+    return [
+        pltpu.VMEM((8, width), f32),
+        pltpu.VMEM((3, 8, width), f32),
+        pltpu.VMEM((2, 8, width), f32),
+        pltpu.VMEM((4, 8, width), f32),
+        pltpu.SemaphoreType.DMA((2, 6)),
+    ]
+
+
+FINISH_PLANS = ((0, D, 0, True), (0, D, D, False), (0, D, 2 * D, True))
+
+
+def statistics(gradient, previous):
+    squares = gradient * gradient + tiny_term
+    rows_new = decay_rate * previous + (1.0 - decay_rate) * jnp.mean(squares, axis=1, keepdims=True)
+    return (
+        rows_new,
+        jnp.sum(squares, axis=0, keepdims=True),
+        jnp.sum(rows_new, axis=0, keepdims=True),
+    )
+
+
+def finish_kernel(scale, *refs):
+    terms, shares = refs[:3], refs[3:6]
+    weights, rows_before, columns_before = refs[6:10], refs[10:14], refs[14:18]
+    gain_two, table_part, gains, moments, own_gains, own_weight = refs[18:24]
+    refs = refs[24:]
+    gradients, updated, rows_after, columns_after = refs[:4], refs[4:8], refs[8:12], refs[12:16]
+    gains_gradient, gains_updated, moments_after, table_total = refs[16:20]
+    scratch = refs[20:]
+    share = scratch[0]
+    early, late = scratch[1:6], scratch[6:11]
+    at = Place()
+    at.greet()
+    scatters = make_scatters(at, FINISH_PLANS, terms, [share] * 3, scratch[11:])
+    first, second = AllSum(at, *early), AllSum(at, *late)
+    for scatter in scatters:
+        scatter.step(0)
+
+    row_counts = [16 * 2 * weight.shape[0] for weight in weights]
+    early_own, late_own = early[0], late[0]
+    early_own[...] = jnp.zeros_like(early_own)
+    late_own[...] = jnp.zeros_like(late_own)
+    rows_new, row_sums = [None] * 4, [None] * 4
+
+    def take(position, raw):
+        gradient = raw * scale
+        gradients[position][...] = gradient
+        rows_new[position], columns, row_sum = statistics(gradient, rows_before[position][...])
+        rows_after[position][...] = rows_new[position]
+        return columns, jnp.broadcast_to(row_sum, (1, 128))
+
+    for position, row in ((1, 0), (2, 1), (3, 2)):
+        columns, row_sum = take(position, shares[position - 1][...])
+        early_own[row : row + 1, D + 128 : D + 256] = row_sum
+        if position == 1:
+            early_own[0:1, :D] = columns
+        elif position == 3:
+            early_own[1:2, :D] = columns
+        else:
+            for part in range(4):
+                early_own[4 + part : 5 + part, :D] = columns[:, D * part : D * part + D]
+    early_own[2:3, :D] = gain_two[...]
+    early_own[:, D : D + 128] = table_part[...]
+
+    def finish(position, columns, row_sum):
+        columns_new = decay_rate * columns_before[position][...] + (1.0 - decay_rate) * (
+            columns / row_counts[position]
+        )
+        columns_after[position][...] = columns_new
+        row_mean = row_sum / row_counts[position]
+        denominator = rows_new[position] * columns_new / row_mean
+        updated[position][...] = weights[position][...] - learn_rate * gradients[position][
+            ...
+        ] * lax.rsqrt(denominator)
+
+    for number in range(5):
+        first.step(number)
+        for scatter in scatters:
+            scatter.step(number + 1)
+
+    raw = share[...]
+    columns, row_sum = take(0, raw)
+    for part in range(3):
+        late_own[part : part + 1, :D] = columns[:, D * part : D * part + D]
+    late_own[4:5, :128] = row_sum
+    gain_one = (
+        jnp.sum(raw * own_weight[...].astype(low_type).astype(f32), axis=1, keepdims=True)
+        / own_gains[...]
+    )
+    rows = gain_one.shape[0]
+    lane = lax.broadcasted_iota(jnp.int32, (rows, D), 1)
+    row = lax.broadcasted_iota(jnp.int32, (rows, D), 0)
+    start = (at.seq * 8 + at.dp) * rows
+    late_own[3:4, :] = jnp.sum(
+        jnp.where(lane == row + start, jnp.broadcast_to(gain_one, (rows, D)), 0.0),
+        axis=0,
+        keepdims=True,
+    )
+    second.step(0)
+    sums = first.total()
+    finish(1, sums[0:1, :D], sums[0:1, D + 128 : D + 129])
+    table_total[...] = sums[:, D : D + 128]
+    second.step(1)
+    finish(3, sums[1:2, :D], sums[2:3, D + 128 : D + 129])
+    second.step(2)
+    finish(
+        2,
+        jnp.concatenate([sums[4 + part : 5 + part, :D] for part in range(4)], axis=1),
+        sums[1:2, D + 128 : D + 129],
+    )
+    second.step(3)
+    second.step(4)
+    sums_late = second.total()
+    finish(
+        0,
+        jnp.concatenate([sums_late[part : part + 1] for part in range(3)], axis=1),
+        sums_late[4:5, 0:1],
+    )
+    gradient = jnp.concatenate([sums_late[3:4], sums[2:3, :D]], axis=0) * scale
+    moment = decay_rate * moments[...] + (1.0 - decay_rate) * (gradient * gradient + tiny_term)
+    gains_gradient[...] = gradient
+    moments_after[...] = moment
+    gains_updated[...] = gains[...] - learn_rate * gradient * lax.rsqrt(moment)
+
+
+def finish(scale, terms, shares, weights, rows_before, columns_before, rest):
+    in_place = pl.BlockSpec(memory_space=pltpu.VMEM)
+    anywhere = pl.BlockSpec(memory_space=pl.ANY)
+    shapes = [weight.shape for weight in weights]
+    out_shapes = (
+        shapes
+        + shapes
+        + [(rows, 1) for rows, _ in shapes]
+        + [(1, columns) for _, columns in shapes]
+        + [(2, D)] * 3
+        + [(8, 128)]
+    )
+    terms = [by_chip(term) for term in terms]
+    return pl.pallas_call(
+        functools.partial(finish_kernel, scale),
+        out_shape=[jax.ShapeDtypeStruct(shape, f32) for shape in out_shapes],
+        in_specs=[anywhere] * 3 + [in_place] * (3 + 12 + 6),
+        out_specs=[in_place] * len(out_shapes),
+        scratch_shapes=[pltpu.VMEM(shapes[0], f32)]
+        + sum_scratch(D + 256)
+        + sum_scratch(D)
+        + scatter_scratch(terms, FINISH_PLANS),
+        compiler_params=pltpu.CompilerParams(
+            collective_id=2, has_side_effects=True, vmem_limit_bytes=vmem_bytes
+        ),
+        cost_estimate=pl.CostEstimate(
+            flops=30 * 10**9, bytes_accessed=30 * 10**6, transcendentals=10**6
+        ),
+        name="finish",
+    )(*terms, *shares, *weights, *rows_before, *columns_before, *rest)
+
+
+BACK_TERMS = (1, 2, 1, 2, 0)
+BACK_PLANS = (
+    (0, 1536, 0, False),
+    (0, 512, 0, True),
+    (1536, 1536, 1536, False),
+    (512, 256, 512, True),
+    (0, D, 0, True),
+)
+EARLY, LATE = (0, 1), (2, 3, 4)
+BACK_TIMES = (
+    (0, None),
+    (0, (EARLY, 0)),
+    (1, (LATE, 0)),
+    (2, (EARLY, 1)),
+    (7, (EARLY, 2)),
+    (7, (LATE, 1)),
+    (12, (EARLY, 3)),
+    (14, (LATE, 2)),
+    (17, (EARLY, 4)),
+    (17, (LATE, 3)),
+    (19, (EARLY, 5)),
+    (22, (LATE, 4)),
+    (23, (LATE, 5)),
+)
+
+
 def backward_kernel(
     queries,
     query_rows,
@@ -192,11 +910,31 @@
     keys,
     values_t,
     keys_extra,
-    query_grad,
-    key_grad_t,
-    value_grad_t,
-    folded,
+    *refs,
 ):
+    if len(refs) > 4:
+        terms, refs = refs[:3], refs[3:]
+        shares, scratch = refs[4:7], refs[7:]
+        at = Place()
+        scatters = make_scatters(
+            at,
+            BACK_PLANS,
+            [terms[which] for which in BACK_TERMS],
+            [shares[which] for which in BACK_TERMS],
+            scratch,
+        )
+        now = pl.program_id(0) * pl.num_programs(1) + pl.program_id(1)
+        for when, doing in BACK_TIMES:
+
+            @pl.when(now == when)
+            def _(doing=doing):
+                if doing is None:
+                    at.greet()
+                else:
+                    for which in doing[0]:
+                        scatters[which].step(doing[1])
+
+    query_grad, key_grad_t, value_grad_t, folded = refs[:4]
     step = pl.program_id(1)
     count, amount = queries.shape[0], keys.shape[0]
     lane = lax.broadcasted_iota(jnp.int32, (count, PAIR), 1)
@@ -216,7 +954,7 @@
         grad_side = jnp.concatenate([jnp.where(mine, grad_pair, zeros), delta_rows[head]], axis=1)
         key_side = jnp.concatenate([keys[...], more], axis=1)
         value_side = jnp.concatenate(
-            [values_t[...], jnp.ones((128, amount), low_type)], axis=0
+            [values_t[0], jnp.ones((128, amount), low_type)], axis=0
         )
         attention = jnp.exp(dot(query_side, key_side, 1, 1))
         score_grad = attention * dot(grad_side, value_side, 1, 0)
@@ -233,8 +971,20 @@
 
 
 def attend_back(
-    queries, query_rows, delta_rows, context_grad, queries_t, context_grad_t, keys, values_t, keys_extra
+    queries,
+    query_rows,
+    delta_rows,
+    context_grad,
+    queries_t,
+    context_grad_t,
+    keys,
+    values_t,
+    keys_extra,
+    terms,
 ):
+    terms = [by_chip(term) for term in terms]
+    anywhere = [pl.BlockSpec(memory_space=pl.ANY)] * len(terms)
+    remote = {"collective_id": 1, "has_side_effects": True} if terms else {}
     count, row_length = queries.shape[0], keys.shape[0]
     blocks = count // BLK
     of_pair = pl.BlockSpec((count, PAIR), lambda pair, step: (0, pair))
@@ -249,7 +999,8 @@
             jax.ShapeDtypeStruct((D, row_length), low_type),
             jax.ShapeDtypeStruct((D, row_length), low_type),
             jax.ShapeDtypeStruct((HEADS, blocks, row_length), f32),
-        ],
+        ]
+        + [jax.ShapeDtypeStruct((term.shape[3] // 2, term.shape[4]), f32) for term in terms],
         in_specs=[
             of_pair,
             of_heads,
@@ -258,16 +1009,21 @@
             of_pair_t,
             of_pair_t,
             pl.BlockSpec((back_step, PAIR), lambda pair, step: (step, pair)),
-            key_t,
+            pl.BlockSpec((1, PAIR, back_step), lambda pair, step: (step, pair, 0)),
             pl.BlockSpec((back_step, 256), lambda pair, step: (step, pair)),
-        ],
+        ]
+        + anywhere,
         out_specs=[
             of_pair,
             key_t,
             key_t,
             pl.BlockSpec((2, blocks, back_step), lambda pair, step: (pair, 0, step)),
-        ],
-        compiler_params=pltpu.CompilerParams(vmem_limit_bytes=vmem_bytes),
+        ]
+        + anywhere,
+        scratch_shapes=scatter_scratch([terms[which] for which in BACK_TERMS], BACK_PLANS)
+        if terms
+        else [],
+        compiler_params=pltpu.CompilerParams(vmem_limit_bytes=vmem_bytes, **remote),
         cost_estimate=pl.CostEstimate(
             flops=10 * HEADS * count * row_length * 200,
             bytes_accessed=HEADS * row_length * 2048,
@@ -284,6 +1040,7 @@
         keys,
         values_t,
         keys_extra,
+        *terms,
     )
 
 
@@ -316,39 +1073,50 @@
     place = lax.axis_index("seq")
     blocks = local_rows // BLK
 
-    project_full = lax.all_gather(project_weight.astype(low_type), every, axis=0, tiled=True)
-    row_states = lax.all_gather(hidden_states[0], "seq", axis=0, tiled=True)
-    mixed = jnp.concatenate([output_weight, expand_weight], axis=1).astype(low_type)
-    mixed_full = lax.all_gather(mixed, every, axis=0, tiled=True)
-    reduce_full = lax.all_gather(reduce_weight.astype(low_type), every, axis=0, tiled=True)
-    output_full, expand_full = mixed_full[:, :D], mixed_full[:, D:]
-
-    doc_all = documents(document_lengths[0], row_length)
-    doc_query = lax.dynamic_slice_in_dim(doc_all, place * local_rows, local_rows)
-    picks = key_picks(bucket_index[0], doc_all, bias_table.shape[0])
-    keys_extra = key_extra(picks, bias_table, blocks)
-    extra = query_extra(doc_query, blocks)
-
+    shards = (project_weight, output_weight, expand_weight, reduce_weight)
+    direct = (
+        lax.axis_size("seq") == 4
+        and lax.axis_size("dp") == 8
+        and all(shard.shape[0] % 8 == 0 and shard.shape[1] % 256 == 0 for shard in shards)
+    )
     inputs = hidden_states[0].astype(f32)
-    normed_one, pullback_one = jax.vjp(rms_norm, inputs, norm_gains[0])
-    normed_low = normed_one.astype(low_type)
-    normed_all = rms_norm(row_states.astype(f32), norm_gains[0]).astype(low_type)
+    if direct:
+        opened = open_layer(
+            shards, hidden_states[0], norm_gains, bucket_index[0], bias_table, document_lengths
+        )
+        project_full, output_full, expand_full, reduce_full = (
+            whole.reshape(-1, whole.shape[4]) for whole in opened[:4]
+        )
+        normed_all, keys = (blocks_of.reshape(row_length, D) for blocks_of in opened[4:6])
+        values_t, keys_extra, queries, queries_t, context_t, log_total, extra = opened[6:]
+        log_total = log_total[:HEADS]
+        normed_low = lax.dynamic_slice_in_dim(normed_all, place * local_rows, local_rows)
+    else:
+        project_full, output_full, expand_full, reduce_full = (
+            lax.all_gather(shard.astype(low_type), every, axis=0, tiled=True) for shard in shards
+        )
+        row_states = lax.all_gather(hidden_states[0], "seq", axis=0, tiled=True)
+        normed_low = rms_norm(inputs, norm_gains[0]).astype(low_type)
+        normed_all = rms_norm(row_states.astype(f32), norm_gains[0]).astype(low_type)
+        doc_all = documents(document_lengths[0], row_length)
+        doc_query = lax.dynamic_slice_in_dim(doc_all, place * local_rows, local_rows)
+        picks = key_picks(bucket_index[0], doc_all, bias_table.shape[0])
+        keys_extra = key_extra(picks, bias_table, blocks)
+        extra = query_extra(doc_query, blocks)
+        scaled = lambda values: (values.astype(low_type).astype(f32) * score_scale).astype(low_type)
+        queries = scaled(dot(normed_low, project_full[:, :D], 1, 0))
+        queries_t = scaled(dot(project_full[:, :D], normed_low, 0, 1))
+        keys = dot(normed_all, project_full[:, D : 2 * D], 1, 0).astype(low_type)
+        values_t = dot(project_full[:, 2 * D :], normed_all, 0, 1).astype(low_type)
+        context_t, log_total = attend(queries, extra, keys, values_t, keys_extra)
+        log_total = log_total.reshape(HEADS, 8, local_rows)[:, 0]
+        values_t = jnp.transpose(values_t.reshape(D, -1, local_rows), (1, 0, 2))
+    _, pullback_one = jax.vjp(rms_norm, inputs, norm_gains[0])
     query_weight, key_weight, value_weight = (
         project_full[:, :D],
         project_full[:, D : 2 * D],
         project_full[:, 2 * D :],
     )
-    queries = (dot(normed_low, query_weight, 1, 0).astype(low_type).astype(f32) * score_scale).astype(
-        low_type
-    )
-    queries_t = (
-        dot(query_weight, normed_low, 0, 1).astype(low_type).astype(f32) * score_scale
-    ).astype(low_type)
-    keys = dot(normed_all, key_weight, 1, 0).astype(low_type)
-    values_t = dot(value_weight, normed_all, 0, 1).astype(low_type)
-
-    context_t, log_total = attend(queries, extra, keys, values_t, keys_extra)
-    log_total = log_total.reshape(HEADS, 8, local_rows)[:, 0]
     context_low_t = context_t.astype(low_type)
     residual = inputs + dot(context_low_t, output_full, 0, 0)
     normed_two, pullback_two = jax.vjp(rms_norm, residual, norm_gains[1])
@@ -374,7 +1142,7 @@
         (context_grad_t.astype(f32) * context_t).reshape(HEADS, HEAD, local_rows), axis=1
     )
 
-    query_grad, key_grad_t, value_grad_t, folded = attend_back(
+    query_grad, key_grad_t, value_grad_t, folded, *rest_shares = attend_back(
         queries,
         with_row_terms(extra, -log_total, blocks),
         with_row_terms(jnp.zeros_like(extra), -delta, blocks),
@@ -384,24 +1152,30 @@
         keys,
         values_t,
         keys_extra,
+        [term.astype(low_type) for term in (output_term, expand_term, reduce_term)]
+        if direct
+        else [],
     )
     buckets = bias_table.shape[0]
+    one_hot = (
+        bucket_index[0].T[:, :, None] == jnp.arange(buckets, dtype=jnp.int32)[None, None, :]
+    ).reshape(row_length, blocks * buckets)
     picked = jnp.dot(
         folded.reshape(HEADS * blocks, row_length),
-        picks[:, : blocks * buckets].astype(f32),
+        one_hot.astype(f32),
         precision=lax.Precision.HIGHEST,
     )
     table_grad = jnp.einsum("hkkb->bh", picked.reshape(HEADS, blocks, blocks, buckets))
 
     query_grad_low = (query_grad * score_scale).astype(low_type)
-    project_term = jnp.concatenate(
-        [
+    project_terms = [
+        term.astype(low_type)
+        for term in (
             dot(normed_low, query_grad_low, 0, 0),
             dot(normed_all, key_grad_t, 0, 1),
             dot(normed_all, value_grad_t, 0, 1),
-        ],
-        axis=1,
-    )
+        )
+    ]
     key_part = dot(key_grad_t, key_weight, 0, 1) + dot(value_grad_t, value_weight, 0, 1)
     key_part = lax.psum_scatter(
         key_part.astype(low_type), "seq", scatter_dimension=0, tiled=True
@@ -409,15 +1183,74 @@
     input_part, gain_one_grad = pullback_one(dot(query_grad_low, query_weight, 1, 1) + key_part)
     input_gradient = (residual_grad + input_part).astype(low_type)[None]
 
-    mixed_term = jnp.concatenate([output_term, expand_term], axis=1).astype(low_type)
-    scatter = lambda term: lax.psum_scatter(
-        term.astype(low_type), every, scatter_dimension=0, tiled=True
-    ).astype(f32)
-    mixed_share = scatter(mixed_term)
-    reduce_share = scatter(reduce_term)
-    project_share = scatter(project_term)
-    shares = (project_share, mixed_share[:, :D], mixed_share[:, D:], reduce_share)
-
+    if direct:
+        rows_of = lambda array: array[:, None]
+        own_rows = project_weight.shape[0]
+        own_gains = lax.dynamic_slice_in_dim(
+            norm_gains[0], (place * lax.axis_size("dp") + lax.axis_index("dp")) * own_rows, own_rows
+        )
+        table_part = jnp.pad(
+            jnp.pad(table_grad, ((0, 0), (0, 16 - HEADS))).reshape(-1, 128), ((0, 4), (0, 0))
+        )
+        results = finish(
+            gradient_scale,
+            project_terms,
+            rest_shares,
+            shards,
+            [rows_of(rows) for rows in (project_rows, output_rows, expand_rows, reduce_rows)],
+            [
+                columns[None]
+                for columns in (project_columns, output_columns, expand_columns, reduce_columns)
+            ],
+            (
+                gain_two_grad[None],
+                table_part,
+                norm_gains,
+                gains_moment,
+                rows_of(own_gains),
+                project_weight,
+            ),
+        )
+        gradients, updated_weights = results[:4], results[4:8]
+        row_after = [rows[:, 0] for rows in results[8:12]]
+        columns_after = [columns[0] for columns in results[12:16]]
+        gains_gradient, gains_updated, gains_moment_new, table_total = results[16:]
+        table_gradient = (
+            table_total[:4].reshape(buckets, 16)[:, :HEADS] * gradient_scale
+        )
+        table_moment_new = decay_rate * table_moment + (1.0 - decay_rate) * (
+            table_gradient * table_gradient + tiny_term
+        )
+        table_updated = bias_table - learn_rate * table_gradient * lax.rsqrt(table_moment_new)
+        return (
+            layer_output,
+            input_gradient,
+            gains_gradient,
+            table_gradient,
+            *gradients,
+            gains_updated,
+            table_updated,
+            *updated_weights,
+            row_after[0],
+            columns_after[0],
+            row_after[1],
+            columns_after[1],
+            row_after[2],
+            columns_after[2],
+            row_after[3],
+            columns_after[3],
+            gains_moment_new,
+            table_moment_new,
+        )
+
+    terms = [
+        term.astype(low_type)
+        for term in (jnp.concatenate(project_terms, axis=1), output_term, expand_term, reduce_term)
+    ]
+    shares = [
+        lax.psum_scatter(term, every, scatter_dimension=0, tiled=True).astype(f32)
+        for term in terms
+    ]
     gradients = tuple((share * gradient_scale for share in shares))
     row_before = (project_rows, output_rows, expand_rows, reduce_rows)
     row_after = []

time: 947 us -> 471 us (0.50)
  waiting for transfers between devices: 530 us -> 0.02 us
  Pallas kernels: 120 us -> 307 us
  matrix products: 134 us -> 90.7 us
  blocking collectives: 41.7 us -> 0 us
  other arithmetic: 58.7 us -> 21.8 us
    reduce_scatter x2 -> x0, waiting for transfers between devices: 221 us -> none  [body(): lax.psum_scatter(term.astype(low_type), every, scatter_dimension=0, tiled...]
    all_gather x4 -> x0, waiting for transfers between devices: 194 us -> none  [the longest x1 85.8 us: body(): row_states = lax.all_gather(hidden_states[0], 'seq', axis=0, tiled=True)]
    pallas_call x1 -> x2, Pallas kernels: 44.8 us -> 219 us  [the longest x1 154 us: open_layer(): pl.pallas_call(opening_kernel, out_shape=[low(*shape) for shape in whole_...]
    reduce_scatter x1, waiting for transfers between devices: 76.5 us -> 0.01 us  [body(): lax.psum_scatter(key_part.astype(low_type), 'seq', scatter_dimension=0, t...]
    dot_general x20 -> x16, matrix products: 129 us -> 86.2 us  [dot(): lax.dot_general(former, latter, (((former_axis,), (latter_axis,)), ((), (...]
    psum x1 -> x0, blocking collectives: 41.7 us -> none  [body(): lax.psum((column_parts[0], column_parts[1], column_parts[2], column_parts...]
    unnamed x9 -> x1, waiting for transfers between devices: 38.6 us -> 0.02 us
    reduce_sum x11 -> x0, other arithmetic: 16.7 us -> none  [the longest x4 6.41 us: body(): row_sums.append(jnp.sum(updated_rows))]
  transfers between devices with their start and end apart: 8 -> 1, of which waited for: 8 -> 0; matrix products, arithmetic and copies ran while one was open for 14% -> 11% of each run, Pallas kernels for 5% -> 14%
where the time goes in v3:
time: 471 us; the launch traced here: 462 us
  Pallas kernels  307 us (65%)
  matrix products  90.7 us (19%)
  local copies, waits for them, and re-layouts  26.7 us (6%)
  other arithmetic  21.8 us (5%)
  between operations  15 us (3%)
    pallas_call x1, Pallas kernels, open_layer(): pl.pallas_call(opening_kernel, out_shape=[low(*shape) for shape in whole_...  154 us
    pallas_call x1, Pallas kernels, attend_back(): pl.pallas_call(backward_kernel, grid=(PAIRS, row_length // back_step), ou...  88.3 us
    dot_general x16, matrix products, dot(): lax.dot_general(former, latter, (((former_axis,), (latter_axis,)), ((), (...  86.2 us
    pallas_call x1, Pallas kernels, finish(): pl.pallas_call(functools.partial(finish_kernel, scale), out_shape=[jax.Sh...  65.5 us
    unnamed x115, local copies, waits for them, and re-layouts  16.7 us
    convert_element_type x1, other arithmetic, with_row_terms(): return result.astype(low_type)  9.53 us
  transfers between devices with their start and end apart: 1, of which 0 were waited for; matrix products, arithmetic and copies ran while one was open for 11% of the time, Pallas kernels for 14%

profile of v3, /device:TPU:0, one launch (start us, length us, event | category | flops | bytes accessed | tf_op | source)
XLA Modules:
  0.0 461.6 jit_solution(6854013355304415278)
XLA Ops:
  7.3 1.6 copy.91
  8.9 1.4 copy.68.refs_7_
  10.3 1.9 slice_reduce_fusion.1
  12.2 153.5 %open_layer.1 = (bf16[4,2,2,48,2304]{4,3,2,1,0:T(8,128)(2,1)}, bf16[4,2,2,48,768]{4,3,2,1,0:T(8,128)(2,1)}, bf16[4,2,2,48,3072]{4,3,2,1,0:T(8,128)(2,1)}, bf16[4...) custom-call(f32[24,2304]{1,0:T(8,128)} %refs_23_.1, ...), custom_call_target="tpu_custom_call" | custom-call | tf_op jit(solution)/shard_map/open_layer/pallas_call | solution.py:617
  165.8 3.4 multiply_reduce_fusion.2
  169.3 6.5 %fusion.45 = f32[768,3072]{1,0:T(8,128)} fusion(bf16[768,3072]{1,0:T(8,128)(2,1)S(1)} %bitcast.113, f32[768,768]{1,0:T(8,128)S(1)} %get-tuple-element.175, f32[768]{0:T(1024)S(1)} %get-tuple-element.157, f32[768]{0:T(1024)S(1)} %fusion.37), kind=kOutput, calls=%fused_computation.95 | convolution fusion | flops 3625648128 | bytes 16521216 | tf_op jit(solution)/shard_map/dot_general | solution.py:34
  175.8 12.5 %fusion.3 = bf16[768,3072]{1,0:T(8,128)(2,1)S(1)} fusion(f32[768,3072]{1,0:T(8,128)} %fusion.45, bf16[3072,768]{1,0:T(8,128)(2,1)S(1)} %bitcast.106, bf16[1,768,768]{2,1,0:T(8,128)(2,1)S(1)} %copy-done.7), kind=kOutput, calls=%fused_computation.7 | convolution fusion | flops 3680501760 | bytes 20054016 | tf_op jit(solution)/shard_map/dot_general | solution.py:34
  188.3 4.1 multiply_reduce_fusion
  194.4 2.2 convert_multiply_fusion.3
  196.6 2.2 convolution_convert_fusion.6.context_grad
  198.8 2.2 convolution_convert_fusion.5
  200.9 5.9 %convolution_convert_fusion.1 = bf16[768,3072]{1,0:T(8,128)(2,1)} fusion(bf16[768,3072]{1,0:T(8,128)(2,1)S(1)} %fusion.3, f32[768,768]{1,0:T(8,128)S(1)} %get-tuple-element.175, f32[768]{0:T(1024)S(1)} %get-tuple-element.157, f32[768]{0:T(1024)S(1)} %fusion.37), kind=kOutput, calls=%fused_computation.18 | convolution fusion | flops 3628007424 | bytes 11802624 | tf_op jit(solution)/shard_map/dot_general | solution.py:34
  206.9 7.0 %convolution_convert_fusion = bf16[3072,768]{1,0:T(8,128)(2,1)} fusion(bf16[1,768,768]{2,1,0:T(8,128)(2,1)S(1)} %copy-done.7, f32[768,3072]{1,0:T(8,128)S(1)} %bitcast.125), kind=kOutput, calls=%fused_computation.17 | convolution fusion | flops 3647471616 | bytes 15335424 | tf_op jit(solution)/shard_map/dot_general | solution.py:34
  214.9 9.5 %select_convert_fusion = (bf16[12,768,128]{2,1,0:T(8,128)(2,1)}, bf16[12,768,128]{2,1,0:T(8,128)(2,1)}) fusion(bf16[12,768]{1,0:T(8,128)(2,1)S(1)} %get-tuple-element.164, bf16[12,768]{1,0:T(8,128)(2,1)S(1)} %get-tuple-element.163, bf16[12,768]{1,0:T(8,128)(2,1)S(1)} %get-tuple-element.162, pred[128]{0:T(512)(128)(4,1)S(1)} %get-tuple-element.183, ...), kind=kLoop, calls=%fused_computation.19 | loop fusion | flops 7077888 | bytes 5026176 | tf_op jit(solution)/shard_map/convert_element_type | solution.py:94
  224.4 88.3 %attention_backward.1 = (f32[768,768]{1,0:T(8,128)}, bf16[768,3072]{1,0:T(8,128)(2,1)}, bf16[768,3072]{1,0:T(8,128)(2,1)}, f32[12,6,3072]{2,1,0:T(8,128)}, f32[2...) custom-call(bf16[768,768]{1,0:T(8,128)(2,1)} %get-tuple-element.68.queries, ...), custom_call_target="tpu_custom_call" | custom-call | flops 56623104000 | bytes 75497472 | tf_op jit(solution)/shard_map/attention_backward/pallas_call | solution.py:994
  312.7 6.0 %fusion.17 = f32[3072,768]{1,0:T(8,128)S(1)} fusion(bf16[768,3072]{1,0:T(8,128)(2,1)} %get-tuple-element.77, bf16[768,2304]{1,0:T(8,128)(2,1)S(1)} %bitcast.116), kind=kOutput, calls=%fused_computation.50 | convolution fusion | flops 3623878656 | bytes 15335424 | tf_op jit(solution)/shard_map/dot_general | solution.py:34
  318.8 6.2 %add_convert_fusion = bf16[3072,768]{1,0:T(8,128)(2,1)} fusion(f32[3072,768]{1,0:T(8,128)S(1)} %fusion.17, bf16[768,3072]{1,0:T(8,128)(2,1)S(1)} %copy-done.38, bf16[768,2304]{1,0:T(8,128)(2,1)S(1)} %bitcast.117), kind=kOutput, calls=%fused_computation.15 | convolution fusion | flops 3628597248 | bytes 20054016 | tf_op jit(solution)/shard_map/dot_general | solution.py:34
  331.2 4.6 fusion.28
  338.1 3.6 convolution_convert_fusion.4
  342.6 4.9 %convolution_convert_fusion.3 = bf16[768,768]{1,0:T(8,128)(2,1)} fusion(bf16[3072,768]{1,0:T(8,128)(2,1)S(1)} %bitcast.110, bf16[768,3072]{1,0:T(8,128)(2,1)S(1)} %copy-done.37), kind=kOutput, calls=%fused_computation.42 | convolution fusion | flops 3624468480 | bytes 10616832 | tf_op jit(solution)/shard_map/dot_general | solution.py:34
  347.5 5.2 %convolution_convert_fusion.2 = bf16[768,768]{1,0:T(8,128)(2,1)} fusion(bf16[3072,768]{1,0:T(8,128)(2,1)S(1)} %bitcast.111, bf16[768,3072]{1,0:T(8,128)(2,1)S(1)} %bitcast.127), kind=kOutput, calls=%fused_computation.41 | convolution fusion | flops 3624468480 | bytes 10616832 | tf_op jit(solution)/shard_map/dot_general | solution.py:34
  352.7 65.5 %finish.1 = (f32[24,2304]{1,0:T(8,128)}, f32[24,768]{1,0:T(8,128)}, f32[24,3072]{1,0:T(8,128)}, f32[96,768]{1,0:T(8,128)}, f32[24,2304]{1,0:T(8,128)}, /*index=5...) custom-call(bf16[4,2,2,48,768]{4,3,2,1,0:T(8,128)(2,1)} %bitcast.121, ...), custom_call_target="tpu_custom_call" | custom-call | flops 30000001024 | bytes 30000000 | tf_op jit(solution)/shard_map/finish/pallas_call | solution.py:858
  420.4 1.3 reduce.2
  421.8 1.3 reduce.3
  423.1 1.3 reduce.4
  424.4 1.3 reduce.5
  425.7 1.3 reduce.6
  427.0 1.4 reduce.7
  428.5 1.3 reduce.8
  430.4 10.4 %fusion.14 = bf16[1,768,768]{2,1,0:T(8,128)(2,1)} fusion(f32[768,768]{1,0:T(8,128)S(1)} %copy-done.6, bf16[3072,768]{1,0:T(8,128)(2,1)} %bitcast.103, f32[768,3072]{1,0:T(8,128)} %fusion.45), kind=kOutput, calls=%fused_computation.47 | convolution fusion | flops 3646291968 | bytes 17694720 | tf_op jit(solution)/shard_map/dot_general | solution.py:34
  440.8 3.8 fusion.12
  444.7 1.6 fusion.15
  (148 shorter events, 23.1 us)
Async XLA Ops:
  7.2 158.6 %copy-start.3 = (bf16[1,768,768]{2,1,0:T(8,128)(2,1)S(1)}, bf16[1,768,768]{2,1,0:T(8,128)(2,1)}, u32[]{:S(2)}) copy-start(bf16[1,768,768]{2,1,0:T(8,128)(2,1)} %param.20) | copy-start | bytes 3538948
  7.2 433.6 %reduce-scatter.2.cloned.1.call-start = ((), (), s32[]{:S(2)}) async-start(), calls=%async_computation.1 | async-start | bytes 5898240 | tf_op jit(solution)/shard_map/reduce_scatter | solution.py:1180
  165.8 10.0 %slice-start = ((s8[4718592]{0:T(1024)(128)(4,1)}), s8[4194304]{0:T(1024)(128)(4,1)S(1)}, s32[]{:S(2)}) async-start(s8[4718592]{0:T(1024)(128)(4,1)} %bitcast.104), calls=%async_computation.2 | async-start | bytes 8388608
  169.2 31.7 %copy-start.5 = (f32[768,768]{1,0:T(8,128)}, f32[768,768]{1,0:T(8,128)S(1)}, u32[]{:S(2)}) copy-start(f32[768,768]{1,0:T(8,128)S(1)} %get-tuple-element.175) | copy-start | bytes 7077892
  169.2 6.5 %copy-start.7 = (bf16[1,768,768]{2,1,0:T(8,128)(2,1)S(1)}, bf16[1,768,768]{2,1,0:T(8,128)(2,1)}, u32[]{:S(2)}) copy-start(bf16[1,768,768]{2,1,0:T(8,128)(2,1)} %param.21) | copy-start | bytes 3538948
  169.3 6.5 %slice-start.1 = ((s8[4718592]{0:T(1024)(128)(4,1)}), s8[524288]{0:T(1024)(128)(4,1)S(1)}, s32[]{:S(2)}) async-start(s8[4718592]{0:T(1024)(128)(4,1)} %bitcast.104), calls=%async_computation.3 | async-start | bytes 1048576
  194.4 4.4 copy-start
  196.6 10.2 %slice-start.4 = ((s8[9437184]{0:T(1024)(128)(4,1)}), s8[4194304]{0:T(1024)(128)(4,1)S(1)}, s32[]{:S(2)}) async-start(s8[9437184]{0:T(1024)(128)(4,1)} %bitcast.124), calls=%async_computation.6 | async-start | bytes 8388608
  198.8 8.1 %slice-start.5 = ((s8[9437184]{0:T(1024)(128)(4,1)}), s8[4194304]{0:T(1024)(128)(4,1)S(1)}, s32[]{:S(2)}) async-start(s8[9437184]{0:T(1024)(128)(4,1)} %bitcast.124), calls=%async_computation.7 | async-start | bytes 8388608
  200.9 5.9 %slice-start.6 = ((s8[9437184]{0:T(1024)(128)(4,1)}), s8[1048576]{0:T(1024)(128)(4,1)S(1)}, s32[]{:S(2)}) async-start(s8[9437184]{0:T(1024)(128)(4,1)} %bitcast.124), calls=%async_computation.8 | async-start | bytes 2097152
  224.4 88.3 %copy-start.35 = (bf16[4,2,2,48,2304]{4,3,2,1,0:T(8,128)(2,1)S(1)}, bf16[4,2,2,48,2304]{4,3,2,1,0:T(8,128)(2,1)}, u32[]{:S(2)}) copy-start(bf16[4,2,2,48,2304]{4,3,2,1,0:T(8,128)(2,1)} %get-tuple-element.76) | copy-start | bytes 10616836
  312.7 6.1 %copy-start.38 = (bf16[768,3072]{1,0:T(8,128)(2,1)S(1)}, bf16[768,3072]{1,0:T(8,128)(2,1)}, u32[]{:S(2)}) copy-start(bf16[768,3072]{1,0:T(8,128)(2,1)} %get-tuple-element.78) | copy-start | bytes 14155780
  325.0 4.6 copy-start.29
  325.0 5.8 %copy-start.9 = (s32[1,6,3072]{2,1,0:T(8,128)S(1)}, s32[1,6,3072]{2,1,0:T(8,128)}, u32[]{:S(2)}) copy-start(s32[1,6,3072]{2,1,0:T(8,128)} %copy.91) | copy-start | bytes 221188
  325.1 16.6 %slice-start.2 = ((s8[4718592]{0:T(1024)(128)(4,1)}), s8[524288]{0:T(1024)(128)(4,1)S(1)}, s32[]{:S(2)}) async-start(s8[4718592]{0:T(1024)(128)(4,1)} %bitcast.108), calls=%async_computation.4 | async-start | bytes 1048576
  325.1 13.0 %copy-start.36 = (f32[768,768]{1,0:T(8,128)S(1)}, f32[768,768]{1,0:T(8,128)}, u32[]{:S(2)}) copy-start(f32[768,768]{1,0:T(8,128)} %get-tuple-element.75) | copy-start | bytes 7077892
  338.1 4.5 copy-start.37
  338.1 9.4 %slice-start.7 = ((s8[4718592]{0:T(1024)(128)(4,1)}), s8[4194304]{0:T(1024)(128)(4,1)S(1)}, s32[]{:S(2)}) async-start(s8[4718592]{0:T(1024)(128)(4,1)} %bitcast.126), calls=%async_computation.9 | async-start | bytes 8388608
  342.6 4.9 %slice-start.8 = ((s8[4718592]{0:T(1024)(128)(4,1)}), s8[524288]{0:T(1024)(128)(4,1)S(1)}, s32[]{:S(2)}) async-start(s8[4718592]{0:T(1024)(128)(4,1)} %bitcast.126), calls=%async_computation.10 | async-start | bytes 1048576
  352.7 66.3 %copy-start.23 = (f32[32,12]{0,1:T(8,128)S(1)}, f32[32,12]{0,1:T(8,128)}, u32[]{:S(2)}) copy-start(f32[32,12]{0,1:T(8,128)} %param.39) | copy-start | bytes 4612
  352.7 66.4 %copy-start.17 = (f32[32,12]{1,0:T(8,128)S(1)}, f32[32,12]{1,0:T(8,128)}, u32[]{:S(2)}) copy-start(f32[32,12]{1,0:T(8,128)} %copy.68.refs_7_) | copy-start | bytes 4612
  352.7 77.7 %copy-start.6 = (f32[768,768]{1,0:T(8,128)S(1)}, f32[768,768]{1,0:T(8,128)}, u32[]{:S(2)}) copy-start(f32[768,768]{1,0:T(8,128)} %copy-done.5) | copy-start | bytes 7077892
  430.4 10.4 %copy-start.4 = (bf16[1,768,768]{2,1,0:T(8,128)(2,1)S(1)}, bf16[1,768,768]{2,1,0:T(8,128)(2,1)}, u32[]{:S(2)}) copy-start(bf16[1,768,768]{2,1,0:T(8,128)(2,1)} %param.20) | copy-start | bytes 3538948
  430.4 10.4 %copy-start.27 = (f32[768]{0:T(1024)S(1)}, f32[768]{0:T(1024)}, u32[]{:S(2)}) copy-start(f32[768]{0:T(1024)} %get-tuple-element.156) | copy-start | bytes 9220
  444.7 4.3 copy-start.12
  444.7 5.0 %copy-start.25 = (f32[2,768]{1,0:T(2,128)S(1)}, f32[2,768]{1,0:T(2,128)}, u32[]{:S(2)}) copy-start(f32[2,768]{1,0:T(2,128)} %get-tuple-element.217) | copy-start | bytes 18436
  444.7 5.6 %copy-start.14 = (f32[24,2304]{1,0:T(8,128)S(1)}, f32[24,2304]{1,0:T(8,128)}, u32[]{:S(2)}) copy-start(f32[24,2304]{1,0:T(8,128)} %get-tuple-element.219) | copy-start | bytes 663556
  444.7 6.3 %copy-start.18 = (f32[24,768]{1,0:T(8,128)S(1)}, f32[24,768]{1,0:T(8,128)}, u32[]{:S(2)}) copy-start(f32[24,768]{1,0:T(8,128)} %get-tuple-element.220) | copy-start | bytes 221188
  446.4 5.3 %copy-start.11 = (f32[24,3072]{1,0:T(8,128)S(1)}, f32[24,3072]{1,0:T(8,128)}, u32[]{:S(2)}) copy-start(f32[24,3072]{1,0:T(8,128)} %get-tuple-element.221) | copy-start | bytes 884740
  446.4 6.0 %copy-start.10 = (f32[96,768]{1,0:T(8,128)S(1)}, f32[96,768]{1,0:T(8,128)}, u32[]{:S(2)}) copy-start(f32[96,768]{1,0:T(8,128)} %get-tuple-element.222) | copy-start | bytes 884740
  446.4 6.7 %copy-start.21 = (f32[1,3072]{1,0:T(1,128)S(1)}, f32[1,3072]{1,0:T(1,128)}, u32[]{:S(2)}) copy-start(f32[1,3072]{1,0:T(1,128)} %get-tuple-element.100) | copy-start | bytes 36868
  446.4 7.3 %copy-start.24 = (f32[2,768]{1,0:T(2,128)S(1)}, f32[2,768]{1,0:T(2,128)}, u32[]{:S(2)}) copy-start(f32[2,768]{1,0:T(2,128)} %get-tuple-element.231) | copy-start | bytes 18436
  (17 other events, 41.0 us)
Sparse Core Ops, SparseCore 0:
  325.2 93.8 reduce-scatter.1
